TPU v7x, 32 devices: a whole 2x2x4 slice. The times are simulated.
32 devices in a mesh: slab: 16 (over z, x, core), half: 2 (over y).
Axes of the slice: x: 2, y: 2, z: 4, core: 2. Of those that a mesh axis runs over, the one named last changes fastest.
Arguments:
- distributions: float32 [19, 32, 32, 256], P(None, 'slab', 'half'), may hold values from 0.02 to 0.1
- cell_states: float32 [2, 3, 169, 3072], P(None, None, None, ('slab', 'half')), may hold values from -6 to 6
- cell_counts: int32 [32], P(('slab', 'half')), may hold values from 16 to 96, as said below
- up_list: int32 [256], P(('slab', 'half')), may hold values from 0 to 96, as said below
- down_list: int32 [256], P(('slab', 'half')), may hold values from 0 to 96, as said below
- spread_sites: int32 [384, 3584], P(None, ('slab', 'half')), may hold values from 0 to 16383
- stiffness: float32 [169], replicated, may hold values from 0.1 to 2
- basis: float32 [169, 384], replicated, may hold values from -0.5 to 0.5
Outputs:
- new_distributions: float32 [19, 32, 32, 256], P(None, 'slab', 'half')
- moved_cells: float32 [2, 3, 169, 3584], P(None, None, None, ('slab', 'half'))
Inputs may be any that keep to these rules, and one draw needn't show every extreme that they name: Each block keeps its cells in its first cell_counts slots. `up_list`: per block, the slots of cells crossing to slab s + 1 (wrapping); live entries come first, are distinct, lie below the block's count and differ from the block's down_list entries; the rest are 96. `down_list`: per block, the slots of cells crossing to slab s - 1 (wrapping); live entries come first, are distinct, lie below the block's count and differ from the block's up_list entries; the rest are 96.
All inputs are finite; a program needn't handle non-finite values.
Results may differ from a plain program's by a relative error of at most 0.0003.
Values sent between devices are 32-bit elements; how exact they have to be, the bound alone decides.
A program may use at most 64 MiB of HBM per device.

v0:
```python
import math

import jax
import jax.numpy as jnp
from jax import lax
from jax.sharding import PartitionSpec as P

full_precision = lax.Precision.HIGHEST
relaxation_time = 0.8
membrane_tension = 0.5
spread_weight = 0.05
lattice_velocities = (
    (0, 0, 0),
    (1, 0, 0),
    (-1, 0, 0),
    (0, 1, 0),
    (0, -1, 0),
    (0, 0, 1),
    (0, 0, -1),
    (1, 1, 0),
    (-1, -1, 0),
    (1, -1, 0),
    (-1, 1, 0),
    (1, 0, 1),
    (-1, 0, -1),
    (1, 0, -1),
    (-1, 0, 1),
    (0, 1, 1),
    (0, -1, -1),
    (0, 1, -1),
    (0, -1, 1),
)
lattice_weights = (1.0 / 3.0,) + (1.0 / 18.0,) * 6 + (1.0 / 36.0,) * 12
opposite_of = (0, 2, 1, 4, 3, 6, 5, 8, 7, 10, 9, 12, 11, 14, 13, 16, 15, 18, 17)


def padded_2(cells, sides, width):
    for axis, dim in sides:
        count = lax.axis_size(axis)
        head = lax.slice_in_dim(cells, 0, width, axis=dim)
        tail = lax.slice_in_dim(cells, cells.shape[dim] - width, cells.shape[dim], axis=dim)
        cells = jnp.concatenate(
            [
                lax.ppermute(tail, axis, [(i, (i + 1) % count) for i in range(count)]),
                cells,
                lax.ppermute(head, axis, [((i + 1) % count, i) for i in range(count)]),
            ],
            axis=dim,
        )
    return cells


def from_behind(array, axis, by):
    devices = lax.axis_size(axis)
    return lax.ppermute(array, axis, [(i, (i + by) % devices) for i in range(devices)])


def point_forces(cells, stiffness, basis):
    current = cells[0]
    rest_shape = cells[1]
    positions = jnp.einsum("kq,ckb->cqb", basis, current, precision=full_precision)
    elastic = jnp.einsum(
        "kq,ckb->cqb",
        basis,
        stiffness[None, :, None] * (rest_shape - current),
        precision=full_precision,
    )
    radial = positions - jnp.mean(positions, axis=1, keepdims=True)
    squared = jnp.sum(radial * radial, axis=0)
    mean_square = jnp.mean(squared, axis=0) + 1e-05
    stretch = squared / mean_square - 1.0
    return elastic - membrane_tension * stretch[None] * radial


def forces_of(cells, stiffness, basis):
    result = point_forces(cells, stiffness, basis)
    return result


def chosen(values, entries, capacity):
    selector = (jnp.arange(capacity, dtype=jnp.int32)[:, None] == entries[None, :]).astype(
        jnp.float32
    )
    return jnp.einsum("...s,sm->...m", values, selector, precision=full_precision)


def spread_points(pushes, spread_sites, site_rows, columns):
    point_rows = pushes.shape[1]
    slot_total = pushes.shape[2]
    group_rows = math.gcd(point_rows, 16)
    row_table = jnp.arange(site_rows, dtype=jnp.int32)
    column_table = jnp.arange(columns, dtype=jnp.int32)

    def visit_rows(turn, total):
        site_piece = lax.dynamic_slice_in_dim(
            spread_sites, turn * group_rows, group_rows, 0
        ).reshape(-1)
        force_piece = lax.dynamic_slice_in_dim(pushes, turn * group_rows, group_rows, 1).reshape(
            3, group_rows * slot_total
        )
        row_hot = (row_table[:, None] == (site_piece // columns)[None, :]).astype(jnp.float32)
        column_hot = ((site_piece % columns)[:, None] == column_table[None, :]).astype(jnp.float32)
        weighted = force_piece[:, None, :] * row_hot[None]
        return total + jnp.einsum("crn,nz->crz", weighted, column_hot, precision=full_precision)

    empty_total = jnp.zeros((3, site_rows, columns), jnp.float32)
    return lax.fori_loop(0, point_rows // group_rows, visit_rows, empty_total)


def collide(populations, force):
    velocity_table = jnp.array(lattice_velocities, jnp.float32)
    weight_table = jnp.array(lattice_weights, jnp.float32)[:, None, None, None]
    density = jnp.sum(populations, axis=0)
    momentum = jnp.einsum("ic,ixyz->cxyz", velocity_table, populations, precision=full_precision)
    flow_speed = (momentum + 0.5 * force) / density
    projected = jnp.einsum("ic,cxyz->ixyz", velocity_table, flow_speed, precision=full_precision)
    force_along = jnp.einsum("ic,cxyz->ixyz", velocity_table, force, precision=full_precision)
    speed_square = jnp.sum(flow_speed * flow_speed, axis=0)
    power_term = jnp.sum(flow_speed * force, axis=0)
    balance = (
        weight_table
        * density
        * (1.0 + 3.0 * projected + 4.5 * projected * projected - 1.5 * speed_square)
    )
    source = weight_table * (3.0 * (force_along - power_term) + 9.0 * projected * force_along)
    return (
        populations
        - (populations - balance) / relaxation_time
        + (1.0 - 0.5 / relaxation_time) * source
    )


def stream_local(relaxed):
    planes = relaxed.shape[1]
    rows_here = relaxed.shape[2]
    row_ids = lax.axis_index("half") * rows_here + jnp.arange(rows_here, dtype=jnp.int32)
    rows_total = rows_here * lax.axis_size("half")
    padded = padded_2(relaxed, (("slab", 1), ("half", 2)), 1)
    shifted = [
        jnp.roll(
            padded[vid, 1 - vel[0] : 1 - vel[0] + planes, 1 - vel[1] : 1 - vel[1] + rows_here],
            vel[2],
            axis=2,
        )
        for vid, vel in enumerate(lattice_velocities)
    ]
    result = []
    for velocity_id, vel in enumerate(lattice_velocities):
        inside = ((row_ids - vel[1] >= 0) & (row_ids - vel[1] < rows_total))[None, :, None]
        result.append(jnp.where(inside, shifted[velocity_id], relaxed[opposite_of[velocity_id]]))
    return jnp.stack(result)


def shards(
    distributions, cell_states, cell_counts, up_list, down_list, spread_sites, stiffness, basis
):
    capacity = cell_states.shape[3]
    planes = distributions.shape[1]
    rows_here = distributions.shape[2]
    columns = distributions.shape[3]
    held_count = cell_counts[0]
    slot_ids = jnp.arange(capacity, dtype=jnp.int32)
    leaving = jnp.concatenate([up_list, down_list])
    keep_mask = (slot_ids < held_count) & ~jnp.any(slot_ids[:, None] == leaving[None, :], axis=1)
    kept_cells = cell_states * keep_mask.astype(jnp.float32)
    from_lower = from_behind(chosen(cell_states, up_list, capacity), "slab", 1)
    from_upper = from_behind(chosen(cell_states, down_list, capacity), "slab", -1)
    moved_cells = jnp.concatenate([kept_cells, from_lower, from_upper], axis=3)
    arriving = point_forces(jnp.concatenate([from_lower, from_upper], axis=3), stiffness, basis)
    pushes = jnp.concatenate([forces_of(kept_cells, stiffness, basis), arriving], axis=2)
    extended = spread_points(pushes, spread_sites, (planes + 2) * rows_here, columns)
    extended = extended.reshape(3, planes + 2, rows_here, columns)
    from_below = from_behind(extended[:, planes + 1], "slab", 1)
    from_above = from_behind(extended[:, 0], "slab", -1)
    summed_force = (
        extended[:, 1 : planes + 1].at[:, 0].add(from_below).at[:, planes - 1].add(from_above)
    )
    force_density = spread_weight * summed_force
    relaxed = collide(distributions, force_density)
    new_distributions = stream_local(relaxed)
    return (new_distributions, moved_cells)


def solution(mesh):
    placed = (
        P(None, "slab", "half", None),
        P(None, None, None, ("slab", "half")),
        P(("slab", "half")),
        P(("slab", "half")),
        P(("slab", "half")),
        P(None, ("slab", "half")),
        P(),
        P(),
    )
    return jax.shard_map(
        shards,
        mesh=mesh,
        in_specs=placed,
        out_specs=(P(None, "slab", "half", None), P(None, None, None, ("slab", "half"))),
        check_vma=False,
    )
```

profile of v0, /device:TPU:0, one launch (start us, length us, event | category | flops | bytes accessed | tf_op | source)
XLA Modules:
  0.0 85.1 jit_solution(1189757146793718548)
XLA Ops:
  0.7 1.7 %convolution_bitcast_fusion.4 = f32[2,3,169,8]{2,3,1,0:T(8,128)S(1)} fusion(f32[2,3,169,96]{3,0,2,1:T(2,128)} %param.17, s32[8]{0:T(128)} %param.20), kind=kOutput, calls=%fused_computation.28 | convolution fusion | flops 9345792 | bytes 421856 | tf_op jit(solution)/shard_map/...s,sm->...m/dot_general | solution.py:84
  2.3 5.4 %collective-permute-start.1 = (f32[2,3,169,8]{2,3,1,0:T(8,128)S(1)}, f32[2,3,169,8]{2,3,1,0:T(8,128)S(1)}, u32[]{:S(2)}, u32[]{:S(2)}) collective-permute-start(f32[2,3,169,8]{2,3,1,0:T(8,128)S(1)} %convolution_bitcast_fusion.4), channel_id=1, source_target_pairs={{0,30},{2,0},{4,2},{6,4},{8,6},{10,8},{12,10},{14,12},{16,14},{18,... | collective-permute-start | bytes 97352 | tf_op jit(solution)/shard_map/ppermute | solution.py:55
  7.8 1.2 %convolution_bitcast_fusion.5 = f32[2,3,169,8]{2,3,1,0:T(8,128)S(1)} fusion(f32[2,3,169,96]{3,0,2,1:T(2,128)S(1)} %copy-done.1, s32[8]{0:T(128)} %param.19), kind=kOutput, calls=%fused_computation.29 | convolution fusion | flops 9345792 | bytes 421856 | tf_op jit(solution)/shard_map/...s,sm->...m/dot_general | solution.py:84
  9.9 0.9 %fusion.63 = (f32[3,96]{1,0:T(4,128)S(1)}, f32[3,384,96]{1,2,0:T(8,128)S(1)}) fusion(f32[169,384]{1,0:T(8,128)S(1)} %copy-done, f32[2,3,169,96]{3,2,1,0:T(8,128)S(1)} %copy_multiply_fusion), kind=kOutput, calls=%fused_computation.179 | convolution fusion | flops 224390880 | bytes 984192 | tf_op jit(solution)/shard_map/kq,ckb->cqb/dot_general | solution.py:61
  10.8 0.2 multiply_reduce_fusion
  11.0 0.1 add_multiply_fusion
  11.2 0.9 %fusion.19 = f32[3,384,96]{1,2,0:T(8,128)S(1)} fusion(f32[3,384,96]{1,2,0:T(8,128)S(1)} %get-tuple-element.273, f32[2,3,169,96]{3,2,1,0:T(8,128)S(1)} %copy_multiply_fusion, f32[169,384]{1,0:T(8,128)S(1)} %copy-done, f32[384,96]{0,1:T(8,128)S(1)} %add_multiply_fusion, f32[3,96]{1,0:T(4,128)S(1)} %broadcast_multiply_fusion.2, f32[169]{0:T(256)S(1)} %copy-done.5), kind=kOutput, calls=%fused_computation.24 | convolution fusion | flops 224709696 | bytes 1682980 | tf_op jit(solution)/shard_map/kq,ckb->cqb/dot_general | solution.py:62
  12.1 0.1 copy.268
  12.2 3.0 %collective-permute-done = f32[2,3,169,8]{2,3,1,0:T(8,128)S(1)} collective-permute-done((f32[2,3,169,8]{2,3,1,0:T(8,128)S(1)}, f32[2,3,169,8]{2,3,1,0:T(8,128)S(1)}, u32[]{:S(2)}, u32[]{:S(2)}) %collective-permute-start) | collective-permute-done | bytes 32480 | tf_op jit(solution)/shard_map/ppermute | solution.py:55
  15.2 0.4 fusion.62
  15.6 0.2 multiply_reduce_fusion.4
  15.9 0.3 fusion.20
  16.3 0.2 copy.267
  16.5 35.8 %while.18 = (s32[]{:T(128)}, f32[3,64,256]{2,1,0:T(8,128)S(1)}, f32[3,384,112]{2,1,0:T(8,128)S(1)}, s32[384,112]{1,0:T(8,128)S(1)}, s32[]{:T(128)}, /*index=5*/s32[]{:T(128)}, s32[]{:T(128)}, s32[]{:T(128)}) while((s32[]{:T(128)}, f32[3,64,256]{2,1,0:T(8,128)S(1)}, f32[3,384,112]{2,1,0:T(8,128)S(1)}, s32[384,112]{1,0:T(8,128)S(1)}, ...), condition=%wide.region_9.10_spmd.clone, body=%wide.region_8.9_spmd.clone.sunk | while | flops 1058129152 | bytes 1482909 | solution.py:107
  16.8 1.2 %fusion.76 = f32[3,64,256]{2,1,0:T(8,128)S(1)} fusion(s32[1792]{0:T(1024)S(1)} %get-tuple-element.317, f32[64,1792]{1,0:T(8,128)S(1)} %fusion.75, f32[3,1792]{1,0:T(4,128)S(1)} %mul.373, f32[3,64,256]{2,1,0:T(8,128)S(1)} %get-tuple-element.328, pred[]{:T(512)S(6)} %compare.30), kind=kOutput, calls=%fused_computation.6.clone.1 | convolution fusion | flops 1057865728 | bytes 880641 | tf_op jit(solution)/shard_map/while/body/eval_jaxpr/crn,nz->crz/dot_general | solution.py:104
  18.2 0.1 mul.373
  18.3 1.2 %fusion.76 = f32[3,64,256]{2,1,0:T(8,128)S(1)} fusion(s32[1792]{0:T(1024)S(1)} %get-tuple-element.317, f32[64,1792]{1,0:T(8,128)S(1)} %fusion.75, f32[3,1792]{1,0:T(4,128)S(1)} %mul.373, f32[3,64,256]{2,1,0:T(8,128)S(1)} %get-tuple-element.328, pred[]{:T(512)S(6)} %compare.30), kind=kOutput, calls=%fused_computation.6.clone.1 | convolution fusion | flops 1057865728 | bytes 880641 | tf_op jit(solution)/shard_map/while/body/eval_jaxpr/crn,nz->crz/dot_general | solution.py:104
  19.6 0.1 mul.373
  19.8 1.2 %fusion.76 = f32[3,64,256]{2,1,0:T(8,128)S(1)} fusion(s32[1792]{0:T(1024)S(1)} %get-tuple-element.317, f32[64,1792]{1,0:T(8,128)S(1)} %fusion.75, f32[3,1792]{1,0:T(4,128)S(1)} %mul.373, f32[3,64,256]{2,1,0:T(8,128)S(1)} %get-tuple-element.328, pred[]{:T(512)S(6)} %compare.30), kind=kOutput, calls=%fused_computation.6.clone.1 | convolution fusion | flops 1057865728 | bytes 880641 | tf_op jit(solution)/shard_map/while/body/eval_jaxpr/crn,nz->crz/dot_general | solution.py:104
  21.3 1.2 %fusion.76 = f32[3,64,256]{2,1,0:T(8,128)S(1)} fusion(s32[1792]{0:T(1024)S(1)} %get-tuple-element.317, f32[64,1792]{1,0:T(8,128)S(1)} %fusion.75, f32[3,1792]{1,0:T(4,128)S(1)} %mul.373, f32[3,64,256]{2,1,0:T(8,128)S(1)} %get-tuple-element.328, pred[]{:T(512)S(6)} %compare.30), kind=kOutput, calls=%fused_computation.6.clone.1 | convolution fusion | flops 1057865728 | bytes 880641 | tf_op jit(solution)/shard_map/while/body/eval_jaxpr/crn,nz->crz/dot_general | solution.py:104
  22.8 1.2 %fusion.76 = f32[3,64,256]{2,1,0:T(8,128)S(1)} fusion(s32[1792]{0:T(1024)S(1)} %get-tuple-element.317, f32[64,1792]{1,0:T(8,128)S(1)} %fusion.75, f32[3,1792]{1,0:T(4,128)S(1)} %mul.373, f32[3,64,256]{2,1,0:T(8,128)S(1)} %get-tuple-element.328, pred[]{:T(512)S(6)} %compare.30), kind=kOutput, calls=%fused_computation.6.clone.1 | convolution fusion | flops 1057865728 | bytes 880641 | tf_op jit(solution)/shard_map/while/body/eval_jaxpr/crn,nz->crz/dot_general | solution.py:104
  24.1 0.1 mul.373
  24.3 1.2 %fusion.76 = f32[3,64,256]{2,1,0:T(8,128)S(1)} fusion(s32[1792]{0:T(1024)S(1)} %get-tuple-element.317, f32[64,1792]{1,0:T(8,128)S(1)} %fusion.75, f32[3,1792]{1,0:T(4,128)S(1)} %mul.373, f32[3,64,256]{2,1,0:T(8,128)S(1)} %get-tuple-element.328, pred[]{:T(512)S(6)} %compare.30), kind=kOutput, calls=%fused_computation.6.clone.1 | convolution fusion | flops 1057865728 | bytes 880641 | tf_op jit(solution)/shard_map/while/body/eval_jaxpr/crn,nz->crz/dot_general | solution.py:104
  25.6 0.1 mul.373
  25.8 1.2 %fusion.76 = f32[3,64,256]{2,1,0:T(8,128)S(1)} fusion(s32[1792]{0:T(1024)S(1)} %get-tuple-element.317, f32[64,1792]{1,0:T(8,128)S(1)} %fusion.75, f32[3,1792]{1,0:T(4,128)S(1)} %mul.373, f32[3,64,256]{2,1,0:T(8,128)S(1)} %get-tuple-element.328, pred[]{:T(512)S(6)} %compare.30), kind=kOutput, calls=%fused_computation.6.clone.1 | convolution fusion | flops 1057865728 | bytes 880641 | tf_op jit(solution)/shard_map/while/body/eval_jaxpr/crn,nz->crz/dot_general | solution.py:104
  27.1 0.1 mul.373
  27.2 1.2 %fusion.76 = f32[3,64,256]{2,1,0:T(8,128)S(1)} fusion(s32[1792]{0:T(1024)S(1)} %get-tuple-element.317, f32[64,1792]{1,0:T(8,128)S(1)} %fusion.75, f32[3,1792]{1,0:T(4,128)S(1)} %mul.373, f32[3,64,256]{2,1,0:T(8,128)S(1)} %get-tuple-element.328, pred[]{:T(512)S(6)} %compare.30), kind=kOutput, calls=%fused_computation.6.clone.1 | convolution fusion | flops 1057865728 | bytes 880641 | tf_op jit(solution)/shard_map/while/body/eval_jaxpr/crn,nz->crz/dot_general | solution.py:104
  28.7 1.2 %fusion.76 = f32[3,64,256]{2,1,0:T(8,128)S(1)} fusion(s32[1792]{0:T(1024)S(1)} %get-tuple-element.317, f32[64,1792]{1,0:T(8,128)S(1)} %fusion.75, f32[3,1792]{1,0:T(4,128)S(1)} %mul.373, f32[3,64,256]{2,1,0:T(8,128)S(1)} %get-tuple-element.328, pred[]{:T(512)S(6)} %compare.30), kind=kOutput, calls=%fused_computation.6.clone.1 | convolution fusion | flops 1057865728 | bytes 880641 | tf_op jit(solution)/shard_map/while/body/eval_jaxpr/crn,nz->crz/dot_general | solution.py:104
  30.2 1.2 %fusion.76 = f32[3,64,256]{2,1,0:T(8,128)S(1)} fusion(s32[1792]{0:T(1024)S(1)} %get-tuple-element.317, f32[64,1792]{1,0:T(8,128)S(1)} %fusion.75, f32[3,1792]{1,0:T(4,128)S(1)} %mul.373, f32[3,64,256]{2,1,0:T(8,128)S(1)} %get-tuple-element.328, pred[]{:T(512)S(6)} %compare.30), kind=kOutput, calls=%fused_computation.6.clone.1 | convolution fusion | flops 1057865728 | bytes 880641 | tf_op jit(solution)/shard_map/while/body/eval_jaxpr/crn,nz->crz/dot_general | solution.py:104
  31.7 1.2 %fusion.76 = f32[3,64,256]{2,1,0:T(8,128)S(1)} fusion(s32[1792]{0:T(1024)S(1)} %get-tuple-element.317, f32[64,1792]{1,0:T(8,128)S(1)} %fusion.75, f32[3,1792]{1,0:T(4,128)S(1)} %mul.373, f32[3,64,256]{2,1,0:T(8,128)S(1)} %get-tuple-element.328, pred[]{:T(512)S(6)} %compare.30), kind=kOutput, calls=%fused_computation.6.clone.1 | convolution fusion | flops 1057865728 | bytes 880641 | tf_op jit(solution)/shard_map/while/body/eval_jaxpr/crn,nz->crz/dot_general | solution.py:104
  33.2 1.2 %fusion.76 = f32[3,64,256]{2,1,0:T(8,128)S(1)} fusion(s32[1792]{0:T(1024)S(1)} %get-tuple-element.317, f32[64,1792]{1,0:T(8,128)S(1)} %fusion.75, f32[3,1792]{1,0:T(4,128)S(1)} %mul.373, f32[3,64,256]{2,1,0:T(8,128)S(1)} %get-tuple-element.328, pred[]{:T(512)S(6)} %compare.30), kind=kOutput, calls=%fused_computation.6.clone.1 | convolution fusion | flops 1057865728 | bytes 880641 | tf_op jit(solution)/shard_map/while/body/eval_jaxpr/crn,nz->crz/dot_general | solution.py:104
  34.7 1.2 %fusion.76 = f32[3,64,256]{2,1,0:T(8,128)S(1)} fusion(s32[1792]{0:T(1024)S(1)} %get-tuple-element.317, f32[64,1792]{1,0:T(8,128)S(1)} %fusion.75, f32[3,1792]{1,0:T(4,128)S(1)} %mul.373, f32[3,64,256]{2,1,0:T(8,128)S(1)} %get-tuple-element.328, pred[]{:T(512)S(6)} %compare.30), kind=kOutput, calls=%fused_computation.6.clone.1 | convolution fusion | flops 1057865728 | bytes 880641 | tf_op jit(solution)/shard_map/while/body/eval_jaxpr/crn,nz->crz/dot_general | solution.py:104
  36.2 1.2 %fusion.76 = f32[3,64,256]{2,1,0:T(8,128)S(1)} fusion(s32[1792]{0:T(1024)S(1)} %get-tuple-element.317, f32[64,1792]{1,0:T(8,128)S(1)} %fusion.75, f32[3,1792]{1,0:T(4,128)S(1)} %mul.373, f32[3,64,256]{2,1,0:T(8,128)S(1)} %get-tuple-element.328, pred[]{:T(512)S(6)} %compare.30), kind=kOutput, calls=%fused_computation.6.clone.1 | convolution fusion | flops 1057865728 | bytes 880641 | tf_op jit(solution)/shard_map/while/body/eval_jaxpr/crn,nz->crz/dot_general | solution.py:104
  37.7 1.2 %fusion.76 = f32[3,64,256]{2,1,0:T(8,128)S(1)} fusion(s32[1792]{0:T(1024)S(1)} %get-tuple-element.317, f32[64,1792]{1,0:T(8,128)S(1)} %fusion.75, f32[3,1792]{1,0:T(4,128)S(1)} %mul.373, f32[3,64,256]{2,1,0:T(8,128)S(1)} %get-tuple-element.328, pred[]{:T(512)S(6)} %compare.30), kind=kOutput, calls=%fused_computation.6.clone.1 | convolution fusion | flops 1057865728 | bytes 880641 | tf_op jit(solution)/shard_map/while/body/eval_jaxpr/crn,nz->crz/dot_general | solution.py:104
  39.2 1.2 %fusion.76 = f32[3,64,256]{2,1,0:T(8,128)S(1)} fusion(s32[1792]{0:T(1024)S(1)} %get-tuple-element.317, f32[64,1792]{1,0:T(8,128)S(1)} %fusion.75, f32[3,1792]{1,0:T(4,128)S(1)} %mul.373, f32[3,64,256]{2,1,0:T(8,128)S(1)} %get-tuple-element.328, pred[]{:T(512)S(6)} %compare.30), kind=kOutput, calls=%fused_computation.6.clone.1 | convolution fusion | flops 1057865728 | bytes 880641 | tf_op jit(solution)/shard_map/while/body/eval_jaxpr/crn,nz->crz/dot_general | solution.py:104
  40.7 1.2 %fusion.76 = f32[3,64,256]{2,1,0:T(8,128)S(1)} fusion(s32[1792]{0:T(1024)S(1)} %get-tuple-element.317, f32[64,1792]{1,0:T(8,128)S(1)} %fusion.75, f32[3,1792]{1,0:T(4,128)S(1)} %mul.373, f32[3,64,256]{2,1,0:T(8,128)S(1)} %get-tuple-element.328, pred[]{:T(512)S(6)} %compare.30), kind=kOutput, calls=%fused_computation.6.clone.1 | convolution fusion | flops 1057865728 | bytes 880641 | tf_op jit(solution)/shard_map/while/body/eval_jaxpr/crn,nz->crz/dot_general | solution.py:104
  42.2 1.2 %fusion.76 = f32[3,64,256]{2,1,0:T(8,128)S(1)} fusion(s32[1792]{0:T(1024)S(1)} %get-tuple-element.317, f32[64,1792]{1,0:T(8,128)S(1)} %fusion.75, f32[3,1792]{1,0:T(4,128)S(1)} %mul.373, f32[3,64,256]{2,1,0:T(8,128)S(1)} %get-tuple-element.328, pred[]{:T(512)S(6)} %compare.30), kind=kOutput, calls=%fused_computation.6.clone.1 | convolution fusion | flops 1057865728 | bytes 880641 | tf_op jit(solution)/shard_map/while/body/eval_jaxpr/crn,nz->crz/dot_general | solution.py:104
  43.7 1.2 %fusion.76 = f32[3,64,256]{2,1,0:T(8,128)S(1)} fusion(s32[1792]{0:T(1024)S(1)} %get-tuple-element.317, f32[64,1792]{1,0:T(8,128)S(1)} %fusion.75, f32[3,1792]{1,0:T(4,128)S(1)} %mul.373, f32[3,64,256]{2,1,0:T(8,128)S(1)} %get-tuple-element.328, pred[]{:T(512)S(6)} %compare.30), kind=kOutput, calls=%fused_computation.6.clone.1 | convolution fusion | flops 1057865728 | bytes 880641 | tf_op jit(solution)/shard_map/while/body/eval_jaxpr/crn,nz->crz/dot_general | solution.py:104
  45.2 1.2 %fusion.76 = f32[3,64,256]{2,1,0:T(8,128)S(1)} fusion(s32[1792]{0:T(1024)S(1)} %get-tuple-element.317, f32[64,1792]{1,0:T(8,128)S(1)} %fusion.75, f32[3,1792]{1,0:T(4,128)S(1)} %mul.373, f32[3,64,256]{2,1,0:T(8,128)S(1)} %get-tuple-element.328, pred[]{:T(512)S(6)} %compare.30), kind=kOutput, calls=%fused_computation.6.clone.1 | convolution fusion | flops 1057865728 | bytes 880641 | tf_op jit(solution)/shard_map/while/body/eval_jaxpr/crn,nz->crz/dot_general | solution.py:104
  46.7 1.2 %fusion.76 = f32[3,64,256]{2,1,0:T(8,128)S(1)} fusion(s32[1792]{0:T(1024)S(1)} %get-tuple-element.317, f32[64,1792]{1,0:T(8,128)S(1)} %fusion.75, f32[3,1792]{1,0:T(4,128)S(1)} %mul.373, f32[3,64,256]{2,1,0:T(8,128)S(1)} %get-tuple-element.328, pred[]{:T(512)S(6)} %compare.30), kind=kOutput, calls=%fused_computation.6.clone.1 | convolution fusion | flops 1057865728 | bytes 880641 | tf_op jit(solution)/shard_map/while/body/eval_jaxpr/crn,nz->crz/dot_general | solution.py:104
  48.2 1.2 %fusion.76 = f32[3,64,256]{2,1,0:T(8,128)S(1)} fusion(s32[1792]{0:T(1024)S(1)} %get-tuple-element.317, f32[64,1792]{1,0:T(8,128)S(1)} %fusion.75, f32[3,1792]{1,0:T(4,128)S(1)} %mul.373, f32[3,64,256]{2,1,0:T(8,128)S(1)} %get-tuple-element.328, pred[]{:T(512)S(6)} %compare.30), kind=kOutput, calls=%fused_computation.6.clone.1 | convolution fusion | flops 1057865728 | bytes 880641 | tf_op jit(solution)/shard_map/while/body/eval_jaxpr/crn,nz->crz/dot_general | solution.py:104
  49.7 1.2 %fusion.76 = f32[3,64,256]{2,1,0:T(8,128)S(1)} fusion(s32[1792]{0:T(1024)S(1)} %get-tuple-element.317, f32[64,1792]{1,0:T(8,128)S(1)} %fusion.75, f32[3,1792]{1,0:T(4,128)S(1)} %mul.373, f32[3,64,256]{2,1,0:T(8,128)S(1)} %get-tuple-element.328, pred[]{:T(512)S(6)} %compare.30), kind=kOutput, calls=%fused_computation.6.clone.1 | convolution fusion | flops 1057865728 | bytes 880641 | tf_op jit(solution)/shard_map/while/body/eval_jaxpr/crn,nz->crz/dot_general | solution.py:104
  51.1 1.2 %fusion.76 = f32[3,64,256]{2,1,0:T(8,128)S(1)} fusion(s32[1792]{0:T(1024)S(1)} %get-tuple-element.317, f32[64,1792]{1,0:T(8,128)S(1)} %fusion.75, f32[3,1792]{1,0:T(4,128)S(1)} %mul.373, f32[3,64,256]{2,1,0:T(8,128)S(1)} %get-tuple-element.328, pred[]{:T(512)S(6)} %compare.30), kind=kOutput, calls=%fused_computation.6.clone.1 | convolution fusion | flops 1057865728 | bytes 880641 | tf_op jit(solution)/shard_map/while/body/eval_jaxpr/crn,nz->crz/dot_general | solution.py:104
  52.4 0.1 copy.269
  52.6 0.8 copy-done.2
  53.5 3.7 %collective-permute-start.3 = (f32[3,16,256]{2,0,1:T(4,128)S(1)}, f32[3,16,256]{2,0,1:T(4,128)S(1)}, u32[]{:S(2)}, u32[]{:S(2)}) collective-permute-start(f32[3,16,256]{2,0,1:T(4,128)S(1)} %get-tuple-element.268), channel_id=1, source_target_pairs={{0,30},{2,0},{4,2},{6,4},{8,6},{10,8},{12,10},{14,12},{16,14},{18,... | collective-permute-start | bytes 147464 | tf_op jit(solution)/shard_map/ppermute | solution.py:55
  57.2 0.2 copy.287
  57.4 0.2 copy.286
  57.6 1.3 %collective-permute-done.2 = f32[3,16,256]{2,0,1:T(4,128)S(1)} collective-permute-done((f32[3,16,256]{2,0,1:T(4,128)S(1)}, f32[3,16,256]{2,0,1:T(4,128)S(1)}, u32[]{:S(2)}, u32[]{:S(2)}) %collective-permute-start.2) | collective-permute-done | bytes 49184 | tf_op jit(solution)/shard_map/ppermute | solution.py:55
  59.1 0.9 %fusion.40 = f32[19,2,16,256]{3,0,2,1:T(8,128)S(1)} fusion(f32[19,3,1,1]{0,1,3,2:T(4,128)S(1)} %copy-done.4, f32[3,2,16,256]{3,0,2,1:T(4,128)S(1)} %fusion.42), kind=kOutput, calls=%fused_computation.60 | convolution fusion | flops 5627904 | bytes 721124 | tf_op jit(solution)/shard_map/ic,cxyz->ixyz/dot_general | solution.py:117
  60.0 1.0 %multiply_reduce_fusion.3 = (f32[2,16,256]{2,1,0:T(8,128)S(1)}, f32[2,16,256]{2,1,0:T(8,128)S(1)}, f32[3,2,16,256]{3,0,2,1:T(4,128)S(1)}) fusion(f32[3,2,16,256]{3,0,2,1:T(4,128)S(1)} %fusion.42, f32[2,16,256]{2,1,0:T(8,128)S(1)} %reduce_sum.81, f32[19,3,1,1]{0,1,3,2:T(4,128)S(1)} %copy-done.4, f32[19,2,16,256]{3,2,1,0:T(8,128)S(1)} %copy-done.2), kind=kOutput, calls=%fused_computation.58 | convolution fusion | flops 5783552 | bytes 917732 | tf_op jit(solution)/shard_map/ic,ixyz->cxyz/dot_general | solution.py:114
  61.1 0.9 %fusion.64 = f32[19,2,16,256]{3,0,2,1:T(8,128)S(1)} fusion(f32[19,3,1,1]{0,1,3,2:T(4,128)S(1)} %copy-done.4, f32[3,2,16,256]{3,0,2,1:T(4,128)S(1)} %get-tuple-element.247), kind=kOutput, calls=%fused_computation.180 | convolution fusion | flops 5603328 | bytes 721124 | tf_op jit(solution)/shard_map/ic,cxyz->ixyz/dot_general | solution.py:116
  61.9 0.6 fusion.29
  62.6 4.5 %collective-permute-start.5 = (f32[19,1,16,256]{3,2,1,0:T(8,128)S(1)}, f32[19,1,16,256]{3,2,1,0:T(8,128)S(1)}, u32[]{:S(2)}, u32[]{:S(2)}) collective-permute-start(f32[19,1,16,256]{3,2,1,0:T(8,128)S(1)} %get-tuple-element.266), channel_id=1, source_target_pairs={{2,0},{4,2},{6,4},{8,6},{10,8},{12,10},{14,12},{16,14},{18,16},{20... | collective-permute-start | bytes 933896 | tf_op jit(solution)/shard_map/ppermute | solution.py:46
  67.1 0.3 pad_maximum_fusion
  67.4 1.1 %copy.288 = f32[2,3,169,112]{3,0,2,1:T(2,128)} copy(f32[2,3,169,112]{3,2,1,0:T(8,128)S(1)} %pad_maximum_fusion) | data formatting | bytes 908544
  68.5 3.0 %collective-permute-done.5 = f32[19,1,16,256]{3,2,1,0:T(8,128)S(1)} collective-permute-done((f32[19,1,16,256]{3,2,1,0:T(8,128)S(1)}, f32[19,1,16,256]{3,2,1,0:T(8,128)S(1)}, u32[]{:S(2)}, u32[]{:S(2)}) %collective-permute-start.5) | collective-permute-done | bytes 311328 | tf_op jit(solution)/shard_map/ppermute | solution.py:46
  71.5 4.6 %collective-permute-done.4 = f32[19,1,16,256]{3,2,1,0:T(8,128)S(1)} collective-permute-done((f32[19,1,16,256]{3,2,1,0:T(8,128)S(1)}, f32[19,1,16,256]{3,2,1,0:T(8,128)S(1)}, u32[]{:S(2)}, u32[]{:S(2)}) %collective-permute-start.4) | collective-permute-done | bytes 311328 | tf_op jit(solution)/shard_map/ppermute | solution.py:44
  76.1 0.1 pad_maximum_fusion.2
  76.2 1.6 %collective-permute-start.7 = (f32[19,4,1,256]{3,2,1,0:T(1,128)S(1)}, f32[19,4,1,256]{3,2,1,0:T(1,128)S(1)}, u32[]{:S(2)}, u32[]{:S(2)}) collective-permute-start(f32[19,4,1,256]{3,2,1,0:T(1,128)S(1)} %get-tuple-element.256), channel_id=1, source_target_pairs={{1,0},{0,1},{3,2},{2,3},{5,4},{4,5},{7,6},{6,7},{9,8},{8,9},{11,10... | collective-permute-start | bytes 233480 | tf_op jit(solution)/shard_map/ppermute | solution.py:46
  77.8 0.5 collective-permute-start.6
  78.5 3.7 %collective-permute-done.6 = f32[19,4,1,256]{3,2,1,0:T(1,128)S(1)} collective-permute-done((f32[19,4,1,256]{3,2,1,0:T(1,128)S(1)}, f32[19,4,1,256]{3,2,1,0:T(1,128)S(1)}, u32[]{:S(2)}, u32[]{:S(2)}) %collective-permute-start.6) | collective-permute-done | bytes 77856 | tf_op jit(solution)/shard_map/ppermute | solution.py:44
  83.6 0.1 constant_dynamic-update-slice_fusion.9
  84.3 0.8 copy-done.6
  (216 shorter events, 8.1 us)
Async XLA Ops:
  0.6 9.3 %copy-start = (f32[169,384]{1,0:T(8,128)S(1)}, f32[169,384]{1,0:T(8,128)}, u32[]{:S(2)}) copy-start(f32[169,384]{1,0:T(8,128)} %param.23) | copy-start | bytes 778756
  0.6 7.1 %copy-start.1 = (f32[2,3,169,96]{3,0,2,1:T(2,128)S(1)}, f32[2,3,169,96]{3,0,2,1:T(2,128)}, u32[]{:S(2)}) copy-start(f32[2,3,169,96]{3,0,2,1:T(2,128)} %param.17) | copy-start | bytes 1168132
  0.7 8.3 %copy-start.9 = (s32[8]{0:T(128)S(1)}, s32[8]{0:T(128)}, u32[]{:S(2)}) copy-start(s32[8]{0:T(128)} %param.20) | copy-start | bytes 100
  0.7 8.3 %copy-start.8 = (s32[8]{0:T(128)S(1)}, s32[8]{0:T(128)}, u32[]{:S(2)}) copy-start(s32[8]{0:T(128)} %param.19) | copy-start | bytes 100
  2.3 12.9 %collective-permute-start.1 = (f32[2,3,169,8]{2,3,1,0:T(8,128)S(1)}, f32[2,3,169,8]{2,3,1,0:T(8,128)S(1)}, u32[]{:S(2)}, u32[]{:S(2)}) collective-permute-start(f32[2,3,169,8]{2,3,1,0:T(8,128)S(1)} %convolution_bitcast_fusion.4), channel_id=1, source_target_pairs={{0,30},{2,0},{4,2},{6,4},{8,6},{10,8},{12,10},{14,12},{16,14},{18,... | collective-permute-start | bytes 97352 | tf_op jit(solution)/shard_map/ppermute | solution.py:55
  9.0 6.2 %collective-permute-start = (f32[2,3,169,8]{2,3,1,0:T(8,128)S(1)}, f32[2,3,169,8]{2,3,1,0:T(8,128)S(1)}, u32[]{:S(2)}, u32[]{:S(2)}) collective-permute-start(f32[2,3,169,8]{2,3,1,0:T(8,128)S(1)} %convolution_bitcast_fusion.5), channel_id=1, source_target_pairs={{0,2},{2,4},{4,6},{6,8},{8,10},{10,12},{12,14},{14,16},{16,18},{18... | collective-permute-start | bytes 97352 | tf_op jit(solution)/shard_map/ppermute | solution.py:55
  9.9 1.2 %copy-start.5 = (f32[169]{0:T(256)S(1)}, f32[169]{0:T(256)}, u32[]{:S(2)}) copy-start(f32[169]{0:T(256)} %param.22) | copy-start | bytes 2032
  11.1 0.9 %copy-start.3 = (s32[384,112]{0,1:T(8,128)S(1)}, s32[384,112]{0,1:T(8,128)}, u32[]{:S(2)}) copy-start(s32[384,112]{0,1:T(8,128)} %param.21) | copy-start | bytes 516100
  52.4 1.1 %copy-start.2 = (f32[19,2,16,256]{3,2,1,0:T(8,128)S(1)}, f32[19,2,16,256]{3,2,1,0:T(8,128)}, u32[]{:S(2)}) copy-start(f32[19,2,16,256]{3,2,1,0:T(8,128)} %param.16) | copy-start | bytes 1867780
  52.6 6.4 %collective-permute-start.2 = (f32[3,16,256]{2,0,1:T(4,128)S(1)}, f32[3,16,256]{2,0,1:T(4,128)S(1)}, u32[]{:S(2)}, u32[]{:S(2)}) collective-permute-start(f32[3,16,256]{2,0,1:T(4,128)S(1)} %get-tuple-element.269), channel_id=1, source_target_pairs={{0,2},{2,4},{4,6},{6,8},{8,10},{10,12},{12,14},{14,16},{16,18},{18... | collective-permute-start | bytes 147464 | tf_op jit(solution)/shard_map/ppermute | solution.py:55
  53.5 5.6 %copy-start.4 = (f32[19,3,1,1]{0,1,3,2:T(4,128)S(1)}, f32[19,3,1,1]{0,1,3,2:T(4,128)}, u32[]{:S(2)}) copy-start(f32[19,3,1,1]{0,1,3,2:T(4,128)} %constant.219) | copy-start | bytes 688
  53.5 5.6 %collective-permute-start.3 = (f32[3,16,256]{2,0,1:T(4,128)S(1)}, f32[3,16,256]{2,0,1:T(4,128)S(1)}, u32[]{:S(2)}, u32[]{:S(2)}) collective-permute-start(f32[3,16,256]{2,0,1:T(4,128)S(1)} %get-tuple-element.268), channel_id=1, source_target_pairs={{0,30},{2,0},{4,2},{6,4},{8,6},{10,8},{12,10},{14,12},{16,14},{18,... | collective-permute-start | bytes 147464 | tf_op jit(solution)/shard_map/ppermute | solution.py:55
  61.0 0.9 %copy-start.7 = (f32[19]{0:T(128)S(1)}, f32[19]{0:T(128)}, u32[]{:S(2)}) copy-start(f32[19]{0:T(128)} %constant.213.clone) | copy-start | bytes 232
  62.6 9.0 %collective-permute-start.5 = (f32[19,1,16,256]{3,2,1,0:T(8,128)S(1)}, f32[19,1,16,256]{3,2,1,0:T(8,128)S(1)}, u32[]{:S(2)}, u32[]{:S(2)}) collective-permute-start(f32[19,1,16,256]{3,2,1,0:T(8,128)S(1)} %get-tuple-element.266), channel_id=1, source_target_pairs={{2,0},{4,2},{6,4},{8,6},{10,8},{12,10},{14,12},{16,14},{18,16},{20... | collective-permute-start | bytes 933896 | tf_op jit(solution)/shard_map/ppermute | solution.py:46
  67.1 9.0 %collective-permute-start.4 = (f32[19,1,16,256]{3,2,1,0:T(8,128)S(1)}, f32[19,1,16,256]{3,2,1,0:T(8,128)S(1)}, u32[]{:S(2)}, u32[]{:S(2)}) collective-permute-start(f32[19,1,16,256]{3,2,1,0:T(8,128)S(1)} %get-tuple-element.267), channel_id=1, source_target_pairs={{0,2},{2,4},{4,6},{6,8},{8,10},{10,12},{12,14},{14,16},{16,18},{18... | collective-permute-start | bytes 933896 | tf_op jit(solution)/shard_map/ppermute | solution.py:44
  76.2 6.1 %collective-permute-start.7 = (f32[19,4,1,256]{3,2,1,0:T(1,128)S(1)}, f32[19,4,1,256]{3,2,1,0:T(1,128)S(1)}, u32[]{:S(2)}, u32[]{:S(2)}) collective-permute-start(f32[19,4,1,256]{3,2,1,0:T(1,128)S(1)} %get-tuple-element.256), channel_id=1, source_target_pairs={{1,0},{0,1},{3,2},{2,3},{5,4},{4,5},{7,6},{6,7},{9,8},{8,9},{11,10... | collective-permute-start | bytes 233480 | tf_op jit(solution)/shard_map/ppermute | solution.py:46
  77.8 4.4 %collective-permute-start.6 = (f32[19,4,1,256]{3,2,1,0:T(1,128)S(1)}, f32[19,4,1,256]{3,2,1,0:T(1,128)S(1)}, u32[]{:S(2)}, u32[]{:S(2)}) collective-permute-start(f32[19,4,1,256]{3,2,1,0:T(1,128)S(1)} %get-tuple-element.257), channel_id=1, source_target_pairs={{0,1},{1,0},{2,3},{3,2},{4,5},{5,4},{6,7},{7,6},{8,9},{9,8},{10,11... | collective-permute-start | bytes 233480 | tf_op jit(solution)/shard_map/ppermute | solution.py:44
  84.2 0.8 copy-start.6
where the time goes:
time: 85.3 us; the launch traced here: 85.1 us
  matrix products  36.8 us (43%)
  starting transfers between devices  15.8 us (19%)
  waiting for transfers between devices  15.8 us (19%)
  local copies, waits for them, and re-layouts  9.02 us (11%)
  other arithmetic  4.62 us (5%)
  between operations  1.64 us (2%)
  loops' own time  1.43 us (2%)
    dot_general x24, matrix products, visit_rows(): jnp.einsum('crn,nz->crz', weighted, column_hot, precision=full_precision)  28.7 us
    ppermute x4, starting transfers between devices, from_behind(): lax.ppermute(array, axis, [(i, (i + by) % devices) for i in range(devices)])  9.18 us
    ppermute x2, waiting for transfers between devices, padded_2(): lax.ppermute(tail, axis, [(i, (i + 1) % count) for i in range(count)])  8.34 us
    ppermute x2, starting transfers between devices, padded_2(): lax.ppermute(head, axis, [((i + 1) % count, i) for i in range(count)])  6.12 us
    ppermute x4, waiting for transfers between devices, from_behind(): lax.ppermute(array, axis, [(i, (i + by) % devices) for i in range(devices)])  4.42 us
    unnamed x25, local copies, waits for them, and re-layouts  3.13 us
    ppermute x2, waiting for transfers between devices, padded_2(): lax.ppermute(head, axis, [((i + 1) % count, i) for i in range(count)])  3.01 us
    dot_general x2, matrix products, chosen(): jnp.einsum('...s,sm->...m', values, selector, precision=full_precision)  2.84 us
  transfers between devices with their start and end apart: 8, of which 6 were waited for; matrix products, arithmetic and copies ran while one was open for 7% of the time, Pallas kernels for 0%

commit v1 on v0

--- a/solution.py
+++ b/solution.py
@@ -87,24 +87,30 @@
 def spread_points(pushes, spread_sites, site_rows, columns):
     point_rows = pushes.shape[1]
     slot_total = pushes.shape[2]
-    group_rows = math.gcd(point_rows, 16)
+    group_rows = math.gcd(point_rows, 32)
     row_table = jnp.arange(site_rows, dtype=jnp.int32)
     column_table = jnp.arange(columns, dtype=jnp.int32)
+    coarse = lax.reduce_precision(pushes, 8, 7)
+    parts = jnp.concatenate([coarse, pushes - coarse], axis=0).astype(jnp.bfloat16)
+    pieces = parts.shape[0]
 
     def visit_rows(turn, total):
         site_piece = lax.dynamic_slice_in_dim(
             spread_sites, turn * group_rows, group_rows, 0
         ).reshape(-1)
-        force_piece = lax.dynamic_slice_in_dim(pushes, turn * group_rows, group_rows, 1).reshape(
-            3, group_rows * slot_total
-        )
-        row_hot = (row_table[:, None] == (site_piece // columns)[None, :]).astype(jnp.float32)
-        column_hot = ((site_piece % columns)[:, None] == column_table[None, :]).astype(jnp.float32)
-        weighted = force_piece[:, None, :] * row_hot[None]
-        return total + jnp.einsum("crn,nz->crz", weighted, column_hot, precision=full_precision)
-
-    empty_total = jnp.zeros((3, site_rows, columns), jnp.float32)
-    return lax.fori_loop(0, point_rows // group_rows, visit_rows, empty_total)
+        force_piece = lax.dynamic_slice_in_dim(parts, turn * group_rows, group_rows, 1).reshape(
+            pieces, group_rows * slot_total
+        )
+        row_hot = row_table[:, None] == (site_piece // columns)[None, :]
+        column_hot = ((site_piece % columns)[:, None] == column_table[None, :]).astype(jnp.bfloat16)
+        weighted = jnp.where(row_hot[None], force_piece[:, None, :], jnp.bfloat16(0))
+        return total + jnp.einsum(
+            "crn,nz->crz", weighted, column_hot, preferred_element_type=jnp.float32
+        )
+
+    empty_total = jnp.zeros((pieces, site_rows, columns), jnp.float32)
+    total = lax.fori_loop(0, point_rows // group_rows, visit_rows, empty_total)
+    return total[: pieces // 2] + total[pieces // 2 :]
 
 
 def collide(populations, force):

time: 85.3 us -> 69 us (0.81)
  matrix products: 36.8 us -> 21.9 us
  local copies, waits for them, and re-layouts: 9.02 us -> 7.56 us
    dot_general x24 -> x12, matrix products: 28.7 us -> 13.9 us  [visit_rows(): jnp.einsum('crn,nz->crz', weighted, column_hot, preferred_element_type=jn...]
    mul x24 -> x0, local copies, waits for them, and re-layouts: 2.22 us -> none  [visit_rows(): weighted = force_piece[:, None, :] * row_hot[None]]
    broadcast_in_dim x0 -> x12, local copies, waits for them, and re-layouts: none -> 1.81 us  [visit_rows(): jnp.where(row_hot[None], force_piece[:, None, :], jnp.bfloat16(0))]
    eq x0 -> x12, other arithmetic: none -> 1.49 us  [visit_rows(): row_hot = row_table[:, None] == (site_piece // columns)[None, :]]
    reshape x24 -> x12, local copies, waits for them, and re-layouts: 1.79 us -> 0.9 us  [visit_rows(): site_piece = lax.dynamic_slice_in_dim(spread_sites, turn * group_rows, gr...]
  transfers between devices with their start and end apart: 8 -> 8, of which waited for: 6 -> 6; matrix products, arithmetic and copies ran while one was open for 7% -> 8% of each run, Pallas kernels for 0% -> 0%
where the time goes in v1:
time: 69 us; the launch traced here: 68.8 us
  matrix products  21.9 us (32%)
  starting transfers between devices  15.8 us (23%)
  waiting for transfers between devices  15.8 us (23%)
  local copies, waits for them, and re-layouts  7.56 us (11%)
  other arithmetic  5.32 us (8%)
  between operations  1.65 us (2%)
  loops' own time  0.73 us (1%)
    dot_general x12, matrix products, visit_rows(): jnp.einsum('crn,nz->crz', weighted, column_hot, preferred_element_type=jn...  13.9 us
    ppermute x4, starting transfers between devices, from_behind(): lax.ppermute(array, axis, [(i, (i + by) % devices) for i in range(devices)])  9.21 us
    ppermute x2, waiting for transfers between devices, padded_2(): lax.ppermute(tail, axis, [(i, (i + 1) % count) for i in range(count)])  8.35 us
    ppermute x2, starting transfers between devices, padded_2(): lax.ppermute(head, axis, [((i + 1) % count, i) for i in range(count)])  6.13 us
    ppermute x4, waiting for transfers between devices, from_behind(): lax.ppermute(array, axis, [(i, (i + by) % devices) for i in range(devices)])  4.42 us
    unnamed x25, local copies, waits for them, and re-layouts  3.19 us
    ppermute x2, waiting for transfers between devices, padded_2(): lax.ppermute(head, axis, [((i + 1) % count, i) for i in range(count)])  3.01 us
    dot_general x2, matrix products, chosen(): jnp.einsum('...s,sm->...m', values, selector, precision=full_precision)  2.84 us
  transfers between devices with their start and end apart: 8, of which 6 were waited for; matrix products, arithmetic and copies ran while one was open for 8% of the time, Pallas kernels for 0%

profile of v1, /device:TPU:0, one launch (start us, length us, event | category | flops | bytes accessed | tf_op | source)
XLA Modules:
  0.0 68.8 jit_solution(10767635213196872879)
XLA Ops:
  0.7 1.7 %convolution_bitcast_fusion.4 = f32[2,3,169,8]{2,3,1,0:T(8,128)S(1)} fusion(f32[2,3,169,96]{3,0,2,1:T(2,128)} %param.17, s32[8]{0:T(128)} %param.20), kind=kOutput, calls=%fused_computation.29 | convolution fusion | flops 9345792 | bytes 421856 | tf_op jit(solution)/shard_map/...s,sm->...m/dot_general | solution.py:84
  2.3 5.4 %collective-permute-start.1 = (f32[2,3,169,8]{2,3,1,0:T(8,128)S(1)}, f32[2,3,169,8]{2,3,1,0:T(8,128)S(1)}, u32[]{:S(2)}, u32[]{:S(2)}) collective-permute-start(f32[2,3,169,8]{2,3,1,0:T(8,128)S(1)} %convolution_bitcast_fusion.4), channel_id=1, source_target_pairs={{0,30},{2,0},{4,2},{6,4},{8,6},{10,8},{12,10},{14,12},{16,14},{18,... | collective-permute-start | bytes 97352 | tf_op jit(solution)/shard_map/ppermute | solution.py:55
  7.8 1.2 %convolution_bitcast_fusion.5 = f32[2,3,169,8]{2,3,1,0:T(8,128)S(1)} fusion(f32[2,3,169,96]{3,0,2,1:T(2,128)S(1)} %copy-done.1, s32[8]{0:T(128)} %param.19), kind=kOutput, calls=%fused_computation.30 | convolution fusion | flops 9345792 | bytes 421856 | tf_op jit(solution)/shard_map/...s,sm->...m/dot_general | solution.py:84
  9.9 0.9 %fusion.65 = (f32[3,96]{1,0:T(4,128)S(1)}, f32[3,384,96]{1,2,0:T(8,128)S(1)}) fusion(f32[169,384]{1,0:T(8,128)S(1)} %copy-done, f32[2,3,169,96]{3,2,1,0:T(8,128)S(1)} %copy_multiply_fusion), kind=kOutput, calls=%fused_computation.185 | convolution fusion | flops 224390880 | bytes 984192 | tf_op jit(solution)/shard_map/kq,ckb->cqb/dot_general | solution.py:61
  10.8 0.2 multiply_reduce_fusion
  11.2 0.9 %fusion.20 = f32[3,384,96]{1,2,0:T(8,128)S(1)} fusion(f32[3,384,96]{1,2,0:T(8,128)S(1)} %get-tuple-element.275, f32[2,3,169,96]{3,2,1,0:T(8,128)S(1)} %copy_multiply_fusion, f32[169,384]{1,0:T(8,128)S(1)} %copy-done, f32[384,96]{0,1:T(8,128)S(1)} %add_multiply_fusion, f32[3,96]{1,0:T(4,128)S(1)} %broadcast_multiply_fusion.2, f32[169]{0:T(256)S(1)} %copy-done.5), kind=kOutput, calls=%fused_computation.25 | convolution fusion | flops 224709696 | bytes 1682980 | tf_op jit(solution)/shard_map/kq,ckb->cqb/dot_general | solution.py:62
  12.2 3.0 %collective-permute-done = f32[2,3,169,8]{2,3,1,0:T(8,128)S(1)} collective-permute-done((f32[2,3,169,8]{2,3,1,0:T(8,128)S(1)}, f32[2,3,169,8]{2,3,1,0:T(8,128)S(1)}, u32[]{:S(2)}, u32[]{:S(2)}) %collective-permute-start) | collective-permute-done | bytes 32480 | tf_op jit(solution)/shard_map/ppermute | solution.py:55
  15.2 0.4 fusion.64
  15.6 0.2 multiply_reduce_fusion.4
  15.9 0.3 fusion.21
  16.4 0.3 copy.268
  16.7 19.3 %while.18 = (s32[]{:T(128)}, f32[6,64,256]{2,1,0:T(8,128)S(1)}, s32[384,112]{1,0:T(8,128)S(1)}, bf16[6,384,112]{2,1,0:T(8,128)(2,1)S(1)}, s32[]{:T(128)}, /*index=5*/s32[]{:T(128)}, s32[]{:T(128)}, s32[]{:T(128)}) while((s32[]{:T(128)}, f32[6,64,256]{2,1,0:T(8,128)S(1)}, s32[384,112]{1,0:T(8,128)S(1)}, ...), condition=%wide.region_9.10_spmd.clone, body=%wide.region_8.9_spmd.clone.sunk | while | flops 707430912 | bytes 1589405 | solution.py:112
  16.9 0.2 broadcast_in_dim.233
  17.0 0.1 iota_compare_fusion.6
  17.1 1.2 %fusion.76 = f32[6,64,256]{2,1,0:T(8,128)S(1)} fusion(s32[3584]{0:T(1024)S(1)} %get-tuple-element.319, pred[64,3584]{1,0:T(8,128)(4,1)S(1)} %iota_compare_fusion.6, bf16[6,3584]{1,0:T(8,128)(2,1)S(1)} %broadcast_in_dim.233, f32[6,64,256]{2,1,0:T(8,128)S(1)} %get-tuple-element.330, pred[]{:T(512)S(6)} %compare.30), kind=kOutput, calls=%fused_computation.10.clone.1 | convolution fusion | flops 707133440 | bytes 1073153 | tf_op jit(solution)/shard_map/while/body/eval_jaxpr/crn,nz->crz/dot_general | solution.py:107
  18.5 0.2 broadcast_in_dim.233
  18.6 0.1 iota_compare_fusion.6
  18.7 1.2 %fusion.76 = f32[6,64,256]{2,1,0:T(8,128)S(1)} fusion(s32[3584]{0:T(1024)S(1)} %get-tuple-element.319, pred[64,3584]{1,0:T(8,128)(4,1)S(1)} %iota_compare_fusion.6, bf16[6,3584]{1,0:T(8,128)(2,1)S(1)} %broadcast_in_dim.233, f32[6,64,256]{2,1,0:T(8,128)S(1)} %get-tuple-element.330, pred[]{:T(512)S(6)} %compare.30), kind=kOutput, calls=%fused_computation.10.clone.1 | convolution fusion | flops 707133440 | bytes 1073153 | tf_op jit(solution)/shard_map/while/body/eval_jaxpr/crn,nz->crz/dot_general | solution.py:107
  20.1 0.2 broadcast_in_dim.233
  20.2 0.1 iota_compare_fusion.6
  20.4 1.2 %fusion.76 = f32[6,64,256]{2,1,0:T(8,128)S(1)} fusion(s32[3584]{0:T(1024)S(1)} %get-tuple-element.319, pred[64,3584]{1,0:T(8,128)(4,1)S(1)} %iota_compare_fusion.6, bf16[6,3584]{1,0:T(8,128)(2,1)S(1)} %broadcast_in_dim.233, f32[6,64,256]{2,1,0:T(8,128)S(1)} %get-tuple-element.330, pred[]{:T(512)S(6)} %compare.30), kind=kOutput, calls=%fused_computation.10.clone.1 | convolution fusion | flops 707133440 | bytes 1073153 | tf_op jit(solution)/shard_map/while/body/eval_jaxpr/crn,nz->crz/dot_general | solution.py:107
  21.7 0.2 broadcast_in_dim.233
  21.8 0.1 iota_compare_fusion.6
  22.0 1.2 %fusion.76 = f32[6,64,256]{2,1,0:T(8,128)S(1)} fusion(s32[3584]{0:T(1024)S(1)} %get-tuple-element.319, pred[64,3584]{1,0:T(8,128)(4,1)S(1)} %iota_compare_fusion.6, bf16[6,3584]{1,0:T(8,128)(2,1)S(1)} %broadcast_in_dim.233, f32[6,64,256]{2,1,0:T(8,128)S(1)} %get-tuple-element.330, pred[]{:T(512)S(6)} %compare.30), kind=kOutput, calls=%fused_computation.10.clone.1 | convolution fusion | flops 707133440 | bytes 1073153 | tf_op jit(solution)/shard_map/while/body/eval_jaxpr/crn,nz->crz/dot_general | solution.py:107
  23.3 0.2 broadcast_in_dim.233
  23.4 0.1 iota_compare_fusion.6
  23.6 1.2 %fusion.76 = f32[6,64,256]{2,1,0:T(8,128)S(1)} fusion(s32[3584]{0:T(1024)S(1)} %get-tuple-element.319, pred[64,3584]{1,0:T(8,128)(4,1)S(1)} %iota_compare_fusion.6, bf16[6,3584]{1,0:T(8,128)(2,1)S(1)} %broadcast_in_dim.233, f32[6,64,256]{2,1,0:T(8,128)S(1)} %get-tuple-element.330, pred[]{:T(512)S(6)} %compare.30), kind=kOutput, calls=%fused_computation.10.clone.1 | convolution fusion | flops 707133440 | bytes 1073153 | tf_op jit(solution)/shard_map/while/body/eval_jaxpr/crn,nz->crz/dot_general | solution.py:107
  24.9 0.2 broadcast_in_dim.233
  25.0 0.1 iota_compare_fusion.6
  25.2 1.2 %fusion.76 = f32[6,64,256]{2,1,0:T(8,128)S(1)} fusion(s32[3584]{0:T(1024)S(1)} %get-tuple-element.319, pred[64,3584]{1,0:T(8,128)(4,1)S(1)} %iota_compare_fusion.6, bf16[6,3584]{1,0:T(8,128)(2,1)S(1)} %broadcast_in_dim.233, f32[6,64,256]{2,1,0:T(8,128)S(1)} %get-tuple-element.330, pred[]{:T(512)S(6)} %compare.30), kind=kOutput, calls=%fused_computation.10.clone.1 | convolution fusion | flops 707133440 | bytes 1073153 | tf_op jit(solution)/shard_map/while/body/eval_jaxpr/crn,nz->crz/dot_general | solution.py:107
  26.5 0.2 broadcast_in_dim.233
  26.7 0.1 iota_compare_fusion.6
  26.8 1.2 %fusion.76 = f32[6,64,256]{2,1,0:T(8,128)S(1)} fusion(s32[3584]{0:T(1024)S(1)} %get-tuple-element.319, pred[64,3584]{1,0:T(8,128)(4,1)S(1)} %iota_compare_fusion.6, bf16[6,3584]{1,0:T(8,128)(2,1)S(1)} %broadcast_in_dim.233, f32[6,64,256]{2,1,0:T(8,128)S(1)} %get-tuple-element.330, pred[]{:T(512)S(6)} %compare.30), kind=kOutput, calls=%fused_computation.10.clone.1 | convolution fusion | flops 707133440 | bytes 1073153 | tf_op jit(solution)/shard_map/while/body/eval_jaxpr/crn,nz->crz/dot_general | solution.py:107
  28.1 0.2 broadcast_in_dim.233
  28.3 0.1 iota_compare_fusion.6
  28.4 1.2 %fusion.76 = f32[6,64,256]{2,1,0:T(8,128)S(1)} fusion(s32[3584]{0:T(1024)S(1)} %get-tuple-element.319, pred[64,3584]{1,0:T(8,128)(4,1)S(1)} %iota_compare_fusion.6, bf16[6,3584]{1,0:T(8,128)(2,1)S(1)} %broadcast_in_dim.233, f32[6,64,256]{2,1,0:T(8,128)S(1)} %get-tuple-element.330, pred[]{:T(512)S(6)} %compare.30), kind=kOutput, calls=%fused_computation.10.clone.1 | convolution fusion | flops 707133440 | bytes 1073153 | tf_op jit(solution)/shard_map/while/body/eval_jaxpr/crn,nz->crz/dot_general | solution.py:107
  29.7 0.2 broadcast_in_dim.233
  29.9 0.1 iota_compare_fusion.6
  30.0 1.2 %fusion.76 = f32[6,64,256]{2,1,0:T(8,128)S(1)} fusion(s32[3584]{0:T(1024)S(1)} %get-tuple-element.319, pred[64,3584]{1,0:T(8,128)(4,1)S(1)} %iota_compare_fusion.6, bf16[6,3584]{1,0:T(8,128)(2,1)S(1)} %broadcast_in_dim.233, f32[6,64,256]{2,1,0:T(8,128)S(1)} %get-tuple-element.330, pred[]{:T(512)S(6)} %compare.30), kind=kOutput, calls=%fused_computation.10.clone.1 | convolution fusion | flops 707133440 | bytes 1073153 | tf_op jit(solution)/shard_map/while/body/eval_jaxpr/crn,nz->crz/dot_general | solution.py:107
  31.3 0.2 broadcast_in_dim.233
  31.6 1.2 %fusion.76 = f32[6,64,256]{2,1,0:T(8,128)S(1)} fusion(s32[3584]{0:T(1024)S(1)} %get-tuple-element.319, pred[64,3584]{1,0:T(8,128)(4,1)S(1)} %iota_compare_fusion.6, bf16[6,3584]{1,0:T(8,128)(2,1)S(1)} %broadcast_in_dim.233, f32[6,64,256]{2,1,0:T(8,128)S(1)} %get-tuple-element.330, pred[]{:T(512)S(6)} %compare.30), kind=kOutput, calls=%fused_computation.10.clone.1 | convolution fusion | flops 707133440 | bytes 1073153 | tf_op jit(solution)/shard_map/while/body/eval_jaxpr/crn,nz->crz/dot_general | solution.py:107
  32.9 0.2 broadcast_in_dim.233
  33.2 1.2 %fusion.76 = f32[6,64,256]{2,1,0:T(8,128)S(1)} fusion(s32[3584]{0:T(1024)S(1)} %get-tuple-element.319, pred[64,3584]{1,0:T(8,128)(4,1)S(1)} %iota_compare_fusion.6, bf16[6,3584]{1,0:T(8,128)(2,1)S(1)} %broadcast_in_dim.233, f32[6,64,256]{2,1,0:T(8,128)S(1)} %get-tuple-element.330, pred[]{:T(512)S(6)} %compare.30), kind=kOutput, calls=%fused_computation.10.clone.1 | convolution fusion | flops 707133440 | bytes 1073153 | tf_op jit(solution)/shard_map/while/body/eval_jaxpr/crn,nz->crz/dot_general | solution.py:107
  34.5 0.2 broadcast_in_dim.233
  34.8 1.2 %fusion.76 = f32[6,64,256]{2,1,0:T(8,128)S(1)} fusion(s32[3584]{0:T(1024)S(1)} %get-tuple-element.319, pred[64,3584]{1,0:T(8,128)(4,1)S(1)} %iota_compare_fusion.6, bf16[6,3584]{1,0:T(8,128)(2,1)S(1)} %broadcast_in_dim.233, f32[6,64,256]{2,1,0:T(8,128)S(1)} %get-tuple-element.330, pred[]{:T(512)S(6)} %compare.30), kind=kOutput, calls=%fused_computation.10.clone.1 | convolution fusion | flops 707133440 | bytes 1073153 | tf_op jit(solution)/shard_map/while/body/eval_jaxpr/crn,nz->crz/dot_general | solution.py:107
  36.0 0.1 copy.269
  36.3 0.8 %copy-done.2 = f32[19,2,16,256]{3,2,1,0:T(8,128)S(1)} copy-done((f32[19,2,16,256]{3,2,1,0:T(8,128)S(1)}, f32[19,2,16,256]{3,2,1,0:T(8,128)}, u32[]{:S(2)}) %copy-start.2) | copy-done | bytes 622616
  37.2 3.7 %collective-permute-start.3 = (f32[3,16,256]{2,0,1:T(4,128)S(1)}, f32[3,16,256]{2,0,1:T(4,128)S(1)}, u32[]{:S(2)}, u32[]{:S(2)}) collective-permute-start(f32[3,16,256]{2,0,1:T(4,128)S(1)} %get-tuple-element.270), channel_id=1, source_target_pairs={{0,30},{2,0},{4,2},{6,4},{8,6},{10,8},{12,10},{14,12},{16,14},{18,... | collective-permute-start | bytes 147464 | tf_op jit(solution)/shard_map/ppermute | solution.py:55
  40.9 0.2 copy.287
  41.1 0.2 copy.286
  41.3 1.3 %collective-permute-done.2 = f32[3,16,256]{2,0,1:T(4,128)S(1)} collective-permute-done((f32[3,16,256]{2,0,1:T(4,128)S(1)}, f32[3,16,256]{2,0,1:T(4,128)S(1)}, u32[]{:S(2)}, u32[]{:S(2)}) %collective-permute-start.2) | collective-permute-done | bytes 49184 | tf_op jit(solution)/shard_map/ppermute | solution.py:55
  42.8 0.9 %fusion.42 = f32[19,2,16,256]{3,0,2,1:T(8,128)S(1)} fusion(f32[19,3,1,1]{0,1,3,2:T(4,128)S(1)} %copy-done.4, f32[3,2,16,256]{3,0,2,1:T(4,128)S(1)} %fusion.44), kind=kOutput, calls=%fused_computation.66 | convolution fusion | flops 5627904 | bytes 721124 | tf_op jit(solution)/shard_map/ic,cxyz->ixyz/dot_general | solution.py:123
  43.7 1.0 %multiply_reduce_fusion.3 = (f32[2,16,256]{2,1,0:T(8,128)S(1)}, f32[2,16,256]{2,1,0:T(8,128)S(1)}, f32[3,2,16,256]{3,0,2,1:T(4,128)S(1)}) fusion(f32[3,2,16,256]{3,0,2,1:T(4,128)S(1)} %fusion.44, f32[2,16,256]{2,1,0:T(8,128)S(1)} %reduce_sum.81, f32[19,3,1,1]{0,1,3,2:T(4,128)S(1)} %copy-done.4, f32[19,2,16,256]{3,2,1,0:T(8,128)S(1)} %copy-done.2), kind=kOutput, calls=%fused_computation.64 | convolution fusion | flops 5783552 | bytes 917732 | tf_op jit(solution)/shard_map/ic,ixyz->cxyz/dot_general | solution.py:120
  44.7 0.9 %fusion.66 = f32[19,2,16,256]{3,0,2,1:T(8,128)S(1)} fusion(f32[19,3,1,1]{0,1,3,2:T(4,128)S(1)} %copy-done.4, f32[3,2,16,256]{3,0,2,1:T(4,128)S(1)} %get-tuple-element.247), kind=kOutput, calls=%fused_computation.186 | convolution fusion | flops 5603328 | bytes 721124 | tf_op jit(solution)/shard_map/ic,cxyz->ixyz/dot_general | solution.py:122
  45.6 0.6 fusion.30
  46.2 4.5 %collective-permute-start.5 = (f32[19,1,16,256]{3,2,1,0:T(8,128)S(1)}, f32[19,1,16,256]{3,2,1,0:T(8,128)S(1)}, u32[]{:S(2)}, u32[]{:S(2)}) collective-permute-start(f32[19,1,16,256]{3,2,1,0:T(8,128)S(1)} %get-tuple-element.266), channel_id=1, source_target_pairs={{2,0},{4,2},{6,4},{8,6},{10,8},{12,10},{14,12},{16,14},{18,16},{20... | collective-permute-start | bytes 933896 | tf_op jit(solution)/shard_map/ppermute | solution.py:46
  50.8 0.3 pad_maximum_fusion
  51.1 1.1 %copy.288 = f32[2,3,169,112]{3,0,2,1:T(2,128)} copy(f32[2,3,169,112]{3,2,1,0:T(8,128)S(1)} %pad_maximum_fusion) | data formatting | bytes 908544
  52.2 3.0 %collective-permute-done.5 = f32[19,1,16,256]{3,2,1,0:T(8,128)S(1)} collective-permute-done((f32[19,1,16,256]{3,2,1,0:T(8,128)S(1)}, f32[19,1,16,256]{3,2,1,0:T(8,128)S(1)}, u32[]{:S(2)}, u32[]{:S(2)}) %collective-permute-start.5) | collective-permute-done | bytes 311328 | tf_op jit(solution)/shard_map/ppermute | solution.py:46
  55.2 4.6 %collective-permute-done.4 = f32[19,1,16,256]{3,2,1,0:T(8,128)S(1)} collective-permute-done((f32[19,1,16,256]{3,2,1,0:T(8,128)S(1)}, f32[19,1,16,256]{3,2,1,0:T(8,128)S(1)}, u32[]{:S(2)}, u32[]{:S(2)}) %collective-permute-start.4) | collective-permute-done | bytes 311328 | tf_op jit(solution)/shard_map/ppermute | solution.py:44
  59.9 1.6 %collective-permute-start.7 = (f32[19,4,1,256]{3,2,1,0:T(1,128)S(1)}, f32[19,4,1,256]{3,2,1,0:T(1,128)S(1)}, u32[]{:S(2)}, u32[]{:S(2)}) collective-permute-start(f32[19,4,1,256]{3,2,1,0:T(1,128)S(1)} %get-tuple-element.256), channel_id=1, source_target_pairs={{1,0},{0,1},{3,2},{2,3},{5,4},{4,5},{7,6},{6,7},{9,8},{8,9},{11,10... | collective-permute-start | bytes 233480 | tf_op jit(solution)/shard_map/ppermute | solution.py:46
  61.5 0.5 collective-permute-start.6
  62.1 3.7 %collective-permute-done.6 = f32[19,4,1,256]{3,2,1,0:T(1,128)S(1)} collective-permute-done((f32[19,4,1,256]{3,2,1,0:T(1,128)S(1)}, f32[19,4,1,256]{3,2,1,0:T(1,128)S(1)}, u32[]{:S(2)}, u32[]{:S(2)}) %collective-permute-start.6) | collective-permute-done | bytes 77856 | tf_op jit(solution)/shard_map/ppermute | solution.py:44
  67.9 0.8 %copy-done.6 = f32[19,2,16,256]{3,2,1,0:T(8,128)} copy-done((f32[19,2,16,256]{3,2,1,0:T(8,128)}, f32[19,2,16,256]{3,2,1,0:T(8,128)S(1)}, u32[]{:S(2)}) %copy-start.6) | copy-done | bytes 622616
  (134 shorter events, 5.2 us)
Async XLA Ops:
  0.6 9.3 %copy-start = (f32[169,384]{1,0:T(8,128)S(1)}, f32[169,384]{1,0:T(8,128)}, u32[]{:S(2)}) copy-start(f32[169,384]{1,0:T(8,128)} %param.23) | copy-start | bytes 778756
  0.6 7.1 %copy-start.1 = (f32[2,3,169,96]{3,0,2,1:T(2,128)S(1)}, f32[2,3,169,96]{3,0,2,1:T(2,128)}, u32[]{:S(2)}) copy-start(f32[2,3,169,96]{3,0,2,1:T(2,128)} %param.17) | copy-start | bytes 1168132
  0.7 8.3 %copy-start.9 = (s32[8]{0:T(128)S(1)}, s32[8]{0:T(128)}, u32[]{:S(2)}) copy-start(s32[8]{0:T(128)} %param.20) | copy-start | bytes 100
  0.7 8.3 %copy-start.8 = (s32[8]{0:T(128)S(1)}, s32[8]{0:T(128)}, u32[]{:S(2)}) copy-start(s32[8]{0:T(128)} %param.19) | copy-start | bytes 100
  2.3 12.9 %collective-permute-start.1 = (f32[2,3,169,8]{2,3,1,0:T(8,128)S(1)}, f32[2,3,169,8]{2,3,1,0:T(8,128)S(1)}, u32[]{:S(2)}, u32[]{:S(2)}) collective-permute-start(f32[2,3,169,8]{2,3,1,0:T(8,128)S(1)} %convolution_bitcast_fusion.4), channel_id=1, source_target_pairs={{0,30},{2,0},{4,2},{6,4},{8,6},{10,8},{12,10},{14,12},{16,14},{18,... | collective-permute-start | bytes 97352 | tf_op jit(solution)/shard_map/ppermute | solution.py:55
  9.0 6.2 %collective-permute-start = (f32[2,3,169,8]{2,3,1,0:T(8,128)S(1)}, f32[2,3,169,8]{2,3,1,0:T(8,128)S(1)}, u32[]{:S(2)}, u32[]{:S(2)}) collective-permute-start(f32[2,3,169,8]{2,3,1,0:T(8,128)S(1)} %convolution_bitcast_fusion.5), channel_id=1, source_target_pairs={{0,2},{2,4},{4,6},{6,8},{8,10},{10,12},{12,14},{14,16},{16,18},{18... | collective-permute-start | bytes 97352 | tf_op jit(solution)/shard_map/ppermute | solution.py:55
  9.9 1.2 %copy-start.5 = (f32[169]{0:T(256)S(1)}, f32[169]{0:T(256)}, u32[]{:S(2)}) copy-start(f32[169]{0:T(256)} %param.22) | copy-start | bytes 2032
  11.1 0.9 %copy-start.3 = (s32[384,112]{0,1:T(8,128)S(1)}, s32[384,112]{0,1:T(8,128)}, u32[]{:S(2)}) copy-start(s32[384,112]{0,1:T(8,128)} %param.21) | copy-start | bytes 516100
  36.0 1.1 %copy-start.2 = (f32[19,2,16,256]{3,2,1,0:T(8,128)S(1)}, f32[19,2,16,256]{3,2,1,0:T(8,128)}, u32[]{:S(2)}) copy-start(f32[19,2,16,256]{3,2,1,0:T(8,128)} %param.16) | copy-start | bytes 1867780
  36.2 6.4 %collective-permute-start.2 = (f32[3,16,256]{2,0,1:T(4,128)S(1)}, f32[3,16,256]{2,0,1:T(4,128)S(1)}, u32[]{:S(2)}, u32[]{:S(2)}) collective-permute-start(f32[3,16,256]{2,0,1:T(4,128)S(1)} %get-tuple-element.271), channel_id=1, source_target_pairs={{0,2},{2,4},{4,6},{6,8},{8,10},{10,12},{12,14},{14,16},{16,18},{18... | collective-permute-start | bytes 147464 | tf_op jit(solution)/shard_map/ppermute | solution.py:55
  37.2 5.7 %copy-start.4 = (f32[19,3,1,1]{0,1,3,2:T(4,128)S(1)}, f32[19,3,1,1]{0,1,3,2:T(4,128)}, u32[]{:S(2)}) copy-start(f32[19,3,1,1]{0,1,3,2:T(4,128)} %constant.226) | copy-start | bytes 688
  37.2 5.6 %collective-permute-start.3 = (f32[3,16,256]{2,0,1:T(4,128)S(1)}, f32[3,16,256]{2,0,1:T(4,128)S(1)}, u32[]{:S(2)}, u32[]{:S(2)}) collective-permute-start(f32[3,16,256]{2,0,1:T(4,128)S(1)} %get-tuple-element.270), channel_id=1, source_target_pairs={{0,30},{2,0},{4,2},{6,4},{8,6},{10,8},{12,10},{14,12},{16,14},{18,... | collective-permute-start | bytes 147464 | tf_op jit(solution)/shard_map/ppermute | solution.py:55
  44.7 0.9 %copy-start.7 = (f32[19]{0:T(128)S(1)}, f32[19]{0:T(128)}, u32[]{:S(2)}) copy-start(f32[19]{0:T(128)} %constant.220.clone) | copy-start | bytes 232
  46.2 9.0 %collective-permute-start.5 = (f32[19,1,16,256]{3,2,1,0:T(8,128)S(1)}, f32[19,1,16,256]{3,2,1,0:T(8,128)S(1)}, u32[]{:S(2)}, u32[]{:S(2)}) collective-permute-start(f32[19,1,16,256]{3,2,1,0:T(8,128)S(1)} %get-tuple-element.266), channel_id=1, source_target_pairs={{2,0},{4,2},{6,4},{8,6},{10,8},{12,10},{14,12},{16,14},{18,16},{20... | collective-permute-start | bytes 933896 | tf_op jit(solution)/shard_map/ppermute | solution.py:46
  50.8 9.0 %collective-permute-start.4 = (f32[19,1,16,256]{3,2,1,0:T(8,128)S(1)}, f32[19,1,16,256]{3,2,1,0:T(8,128)S(1)}, u32[]{:S(2)}, u32[]{:S(2)}) collective-permute-start(f32[19,1,16,256]{3,2,1,0:T(8,128)S(1)} %get-tuple-element.267), channel_id=1, source_target_pairs={{0,2},{2,4},{4,6},{6,8},{8,10},{10,12},{12,14},{14,16},{16,18},{18... | collective-permute-start | bytes 933896 | tf_op jit(solution)/shard_map/ppermute | solution.py:44
  59.9 6.1 %collective-permute-start.7 = (f32[19,4,1,256]{3,2,1,0:T(1,128)S(1)}, f32[19,4,1,256]{3,2,1,0:T(1,128)S(1)}, u32[]{:S(2)}, u32[]{:S(2)}) collective-permute-start(f32[19,4,1,256]{3,2,1,0:T(1,128)S(1)} %get-tuple-element.256), channel_id=1, source_target_pairs={{1,0},{0,1},{3,2},{2,3},{5,4},{4,5},{7,6},{6,7},{9,8},{8,9},{11,10... | collective-permute-start | bytes 233480 | tf_op jit(solution)/shard_map/ppermute | solution.py:46
  61.5 4.4 %collective-permute-start.6 = (f32[19,4,1,256]{3,2,1,0:T(1,128)S(1)}, f32[19,4,1,256]{3,2,1,0:T(1,128)S(1)}, u32[]{:S(2)}, u32[]{:S(2)}) collective-permute-start(f32[19,4,1,256]{3,2,1,0:T(1,128)S(1)} %get-tuple-element.257), channel_id=1, source_target_pairs={{0,1},{1,0},{2,3},{3,2},{4,5},{5,4},{6,7},{7,6},{8,9},{9,8},{10,11... | collective-permute-start | bytes 233480 | tf_op jit(solution)/shard_map/ppermute | solution.py:44
  67.9 0.8 %copy-start.6 = (f32[19,2,16,256]{3,2,1,0:T(8,128)}, f32[19,2,16,256]{3,2,1,0:T(8,128)S(1)}, u32[]{:S(2)}) copy-start(f32[19,2,16,256]{3,2,1,0:T(8,128)S(1)} %constant_dynamic-update-slice_fusion.2) | copy-start | bytes 1867780

commit v2 on v0

v2 whole, which is shorter than its diff:
```python
import jax
import jax.numpy as jnp
from jax import lax
from jax.experimental import pallas as pl
from jax.experimental.pallas import tpu as pltpu
from jax.sharding import PartitionSpec as P

full_precision = lax.Precision.HIGHEST
relaxation_time = 0.8
membrane_tension = 0.5
spread_weight = 0.05
lattice_velocities = (
    (0, 0, 0),
    (1, 0, 0),
    (-1, 0, 0),
    (0, 1, 0),
    (0, -1, 0),
    (0, 0, 1),
    (0, 0, -1),
    (1, 1, 0),
    (-1, -1, 0),
    (1, -1, 0),
    (-1, 1, 0),
    (1, 0, 1),
    (-1, 0, -1),
    (1, 0, -1),
    (-1, 0, 1),
    (0, 1, 1),
    (0, -1, -1),
    (0, 1, -1),
    (0, -1, 1),
)
lattice_weights = (1.0 / 3.0,) + (1.0 / 18.0,) * 6 + (1.0 / 36.0,) * 12
opposite_of = (0, 2, 1, 4, 3, 6, 5, 8, 7, 10, 9, 12, 11, 14, 13, 16, 15, 18, 17)
all_ids = tuple(range(19))
ahead_ids = tuple(i for i in all_ids if lattice_velocities[i][0] == 1)
behind_ids = tuple(i for i in all_ids if lattice_velocities[i][0] == -1)
rising_ids = tuple(i for i in all_ids if lattice_velocities[i][1] == 1)
falling_ids = tuple(opposite_of[i] for i in rising_ids)
level_ids = tuple(i for i in all_ids if lattice_velocities[i][1] == 0)


def total_of(terms):
    result = None
    for sign, value in terms:
        if sign == 0:
            continue
        if result is None:
            result = value if sign > 0 else -value
        else:
            result = result + value if sign > 0 else result - value
    return result


def moments_of(populations):
    density = total_of([(1, f) for f in populations])
    momentum = [
        total_of([(lattice_velocities[i][axis], populations[i]) for i in all_ids])
        for axis in range(3)
    ]
    return [density] + momentum


def collide(ids, population_of, moments, force):
    density = moments[0]
    inverse = 1.0 / density
    speed = [(moments[1 + a] + 0.5 * force[a]) * inverse for a in range(3)]
    speed_square = speed[0] * speed[0] + speed[1] * speed[1] + speed[2] * speed[2]
    power = speed[0] * force[0] + speed[1] * force[1] + speed[2] * force[2]
    base = 1.0 - 1.5 * speed_square
    result = {}
    for i in ids:
        vel = lattice_velocities[i]
        weight = lattice_weights[i]
        f = population_of(i)
        if i == 0:
            balance = (weight * density) * base
            source = (-3.0 * weight) * power
        else:
            projected = total_of(list(zip(vel, speed)))
            along = total_of(list(zip(vel, force)))
            balance = (weight * density) * (base + projected * (3.0 + 4.5 * projected))
            source = weight * (3.0 * (along - power) + 9.0 * projected * along)
        result[i] = (
            f - (f - balance) / relaxation_time + (1.0 - 0.5 / relaxation_time) * source
        )
    return result


def step_kernel(
    count_ref,
    up_ref,
    down_ref,
    dist_ref,
    cells_ref,
    sites_ref,
    stiff_ref,
    basis_ref,
    out_ref,
    moved_ref,
    basis_pad,
    stiff_pad,
    pushes,
    spread_acc,
    cell_send,
    cell_recv,
    halo_send,
    halo_recv,
    force_own,
    force_recv,
    row_send,
    row_recv,
    own_moments,
    relaxed,
    send_sems,
    recv_sems,
):
    slab = lax.axis_index("slab")
    half = lax.axis_index("half")
    slabs = lax.axis_size("slab")
    above = {"slab": lax.rem(slab + 1, slabs), "half": half}
    below = {"slab": lax.rem(slab + slabs - 1, slabs), "half": half}
    across = {"slab": slab, "half": 1 - half}
    mesh_ids = pl.DeviceIdType.MESH

    planes, rows, columns = dist_ref.shape[1:]
    coefficients, points = basis_ref.shape
    capacity, width = cells_ref.shape[2:]
    move = up_ref.shape[0]
    slots = sites_ref.shape[0]

    barrier = pltpu.get_barrier_semaphore()
    for device in (above, below, across):
        pl.semaphore_signal(barrier, inc=1, device_id=device, device_id_type=mesh_ids)

    def remote(at, source, target, device):
        return pltpu.make_async_remote_copy(
            src_ref=source,
            dst_ref=target,
            send_sem=send_sems.at[at],
            recv_sem=recv_sems.at[at],
            device_id=device,
            device_id_type=mesh_ids,
        )

    entry_ids = lax.broadcasted_iota(jnp.int32, (2 * move, capacity), 0)
    slot_ids = lax.broadcasted_iota(jnp.int32, (2 * move, capacity), 1)
    entries = jnp.zeros((2 * move, capacity), jnp.int32)
    for k in range(move):
        entries = jnp.where(entry_ids == k, up_ref[k], entries)
        entries = jnp.where(entry_ids == move + k, down_ref[k], entries)
    selector = (entries == slot_ids).astype(jnp.float32)
    for w in range(2):
        for c in range(3):
            picked = jnp.dot(
                selector,
                cells_ref[w, c],
                precision=full_precision,
                preferred_element_type=jnp.float32,
            )
            cell_send[0, w, c] = picked[:move]
            cell_send[1, w, c] = picked[move:]

    pl.semaphore_wait(barrier, 3)
    cells_up = remote(0, cell_send.at[0], cell_recv.at[0], above)
    cells_down = remote(1, cell_send.at[1], cell_recv.at[1], below)
    cells_up.start()
    cells_down.start()

    for p in range(planes):
        moments = moments_of([dist_ref[i, p] for i in all_ids])
        for k in range(4):
            own_moments[k, p] = moments[k]
    for side, (p, ids) in enumerate(((planes - 1, ahead_ids), (0, behind_ids))):
        for k in range(4):
            halo_send[side, k] = own_moments[k, p]
        for k, i in enumerate(ids):
            halo_send[side, 4 + k] = dist_ref[i, p]
    halo_up = remote(2, halo_send.at[0], halo_recv.at[0], above)
    halo_down = remote(3, halo_send.at[1], halo_recv.at[1], below)
    halo_up.start()
    halo_down.start()

    basis_pad[...] = jnp.zeros_like(basis_pad)
    basis_pad[:coefficients, :] = basis_ref[...]
    stiff_pad[...] = jnp.zeros_like(stiff_pad)
    stiff_pad[:, :coefficients] = stiff_ref[...]

    held = lax.broadcasted_iota(jnp.int32, (capacity, width), 0)
    gone = held >= count_ref[0]
    for k in range(move):
        gone = gone | (held == up_ref[k]) | (held == down_ref[k])
    for w in range(2):
        for c in range(3):
            moved_ref[w, c, :capacity, :] = jnp.where(gone, 0.0, cells_ref[w, c])

    def point_forces(first, count):
        current = [moved_ref[0, c, first : first + count, :] for c in range(3)]
        rest = [moved_ref[1, c, first : first + count, :] for c in range(3)]
        stiffness = stiff_pad[...]
        strain = [stiffness * (r - x) for r, x in zip(rest, current)]
        product = jnp.dot(
            jnp.concatenate(current + strain, axis=0),
            basis_pad[...],
            precision=full_precision,
            preferred_element_type=jnp.float32,
        )
        parts = [product[k * count : (k + 1) * count] for k in range(6)]
        radial = [x - jnp.sum(x, axis=1, keepdims=True) / points for x in parts[:3]]
        squared = radial[0] * radial[0] + radial[1] * radial[1] + radial[2] * radial[2]
        mean_square = jnp.sum(squared, axis=1, keepdims=True) / points + 1e-05
        factor = membrane_tension * (squared / mean_square - 1.0)
        for c in range(3):
            pushes[c, first : first + count, :] = parts[3 + c] - factor * radial[c]

    group = 8
    site_rows = spread_acc.shape[0] // 6
    shift = columns.bit_length() - 1
    zero = jnp.zeros((), jnp.bfloat16)

    def spread(turn, carry):
        start = pl.multiple_of(turn * group, group)
        sites = sites_ref[pl.ds(start, group), :]
        row_of = (sites >> shift).astype(jnp.float32)
        column_of = (sites & (columns - 1)).astype(jnp.float32)
        values = []
        for c in range(3):
            push = pushes[c, pl.ds(start, group), :]
            coarse = push.astype(jnp.bfloat16).astype(jnp.float32)
            values += [coarse, push - coarse]
        row_ids = lax.broadcasted_iota(jnp.int32, (site_rows, points), 0)
        row_ids = row_ids.astype(jnp.float32).astype(jnp.bfloat16)
        column_ids = lax.broadcasted_iota(jnp.int32, (columns, points), 0)
        column_ids = column_ids.astype(jnp.float32).astype(jnp.bfloat16)

        def tall(array, k, height):
            tile = jnp.broadcast_to(array[k : k + 1], (16, points)).astype(jnp.bfloat16)
            return jnp.concatenate([tile] * (height // 16), axis=0)

        weighted = []
        hot = []
        for k in range(group):
            mask = row_ids == tall(row_of, k, site_rows)
            weighted.append(
                jnp.concatenate(
                    [jnp.where(mask, tall(v, k, site_rows), zero) for v in values], axis=0
                )
            )
            hot.append(
                jnp.where(
                    column_ids == tall(column_of, k, columns), jnp.ones((), jnp.bfloat16), zero
                )
            )
        spread_acc[...] += lax.dot_general(
            jnp.concatenate(weighted, axis=1),
            jnp.concatenate(hot, axis=1),
            (((1,), (1,)), ((), ())),
            preferred_element_type=jnp.float32,
        )
        return carry

    spread_acc[...] = jnp.zeros_like(spread_acc)
    point_forces(0, capacity)
    lax.fori_loop(0, capacity // group, spread, 0)

    cells_up.wait()
    cells_down.wait()
    for w in range(2):
        for c in range(3):
            moved_ref[w, c, capacity : capacity + move, :] = cell_recv[0, w, c]
            moved_ref[w, c, capacity + move :, :] = cell_recv[1, w, c]
    point_forces(capacity, 2 * move)
    lax.fori_loop(capacity // group, slots // group, spread, 0)

    for c in range(3):
        first = 2 * c * site_rows
        whole = spread_acc[first : first + site_rows, :] + (
            spread_acc[first + site_rows : first + 2 * site_rows, :]
        )
        whole = (spread_weight * whole).reshape(2, 2, rows, columns)
        force_own[0, c] = whole[0]
        force_own[1, c] = whole[1]
    force_down = remote(4, force_own.at[0], force_recv.at[1], below)
    force_up = remote(5, force_own.at[1], force_recv.at[0], above)
    force_down.start()
    force_up.start()
    halo_up.wait()
    halo_down.wait()
    force_down.wait()
    force_up.wait()

    for plane in range(planes + 2):
        side, at = divmod(plane, 2)
        force = [force_own[side, c, at] + force_recv[side, c, at] for c in range(3)]
        if plane == 0 or plane == planes + 1:
            which = 0 if plane == 0 else 1
            ids = ahead_ids if plane == 0 else behind_ids
            moments = [halo_recv[which, k] for k in range(4)]
            found = collide(
                ids, lambda i: halo_recv[which, 4 + ids.index(i)], moments, force
            )
        else:
            moments = [own_moments[k, plane - 1] for k in range(4)]
            found = collide(all_ids, lambda i: dist_ref[i, plane - 1], moments, force)
        for i, value in found.items():
            relaxed[i, plane] = value

    def carried(i, p):
        vel = lattice_velocities[i]
        value = relaxed[i, p + 1 - vel[0]]
        if vel[2]:
            value = pltpu.roll(value, vel[2] % columns, 1)
        return value

    row_ids = lax.broadcasted_iota(jnp.int32, (rows, columns), 0)
    lower_half = jnp.full((1, columns), half, jnp.int32) == 0
    for j, (i, o) in enumerate(zip(rising_ids, falling_ids)):
        for p in range(planes):
            rising = carried(i, p)
            falling = carried(o, p)
            at = j * planes + p
            row_send[at : at + 1, :] = jnp.where(lower_half, rising[rows - 1 :], falling[:1])
            out_ref[i, p] = jnp.where(row_ids == 0, relaxed[o, p + 1], pltpu.roll(rising, 1, 0))
            out_ref[o, p] = jnp.where(
                row_ids == rows - 1, relaxed[i, p + 1], pltpu.roll(falling, rows - 1, 0)
            )
    rows_across = remote(6, row_send, row_recv, across)
    rows_across.start()
    for i in level_ids:
        for p in range(planes):
            out_ref[i, p] = carried(i, p)
    rows_across.wait()

    @pl.when(half == 0)
    def _():
        for j, i in enumerate(falling_ids):
            for p in range(planes):
                at = j * planes + p
                out_ref[i, p, rows - 1 :, :] = row_recv[at : at + 1, :]

    @pl.when(half != 0)
    def _():
        for j, i in enumerate(rising_ids):
            for p in range(planes):
                at = j * planes + p
                out_ref[i, p, :1, :] = row_recv[at : at + 1, :]


def shards(
    distributions, cell_states, cell_counts, up_list, down_list, spread_sites, stiffness, basis
):
    coefficients = cell_states.shape[2]
    capacity = cell_states.shape[3]
    planes, rows, columns = distributions.shape[1:]
    points, slots = spread_sites.shape
    move = up_list.shape[0]
    width = -(-coefficients // 128) * 128
    cells = jnp.pad(
        jnp.transpose(cell_states, (0, 1, 3, 2)),
        ((0, 0), (0, 0), (0, 0), (0, width - coefficients)),
    )
    scalars = pl.BlockSpec(memory_space=pltpu.SMEM)
    vectors = pl.BlockSpec(memory_space=pltpu.VMEM)
    f32 = jnp.float32
    new_distributions, moved = pl.pallas_call(
        step_kernel,
        out_shape=(
            jax.ShapeDtypeStruct(distributions.shape, f32),
            jax.ShapeDtypeStruct((2, 3, slots, width), f32),
        ),
        in_specs=[scalars] * 3 + [vectors] * 5,
        out_specs=(vectors, vectors),
        scratch_shapes=[
            pltpu.VMEM((width, points), f32),
            pltpu.VMEM((1, width), f32),
            pltpu.VMEM((3, slots, points), f32),
            pltpu.VMEM((6 * (planes + 2) * rows, columns), f32),
            pltpu.VMEM((2, 2, 3, move, width), f32),
            pltpu.VMEM((2, 2, 3, move, width), f32),
            pltpu.VMEM((2, 9, rows, columns), f32),
            pltpu.VMEM((2, 9, rows, columns), f32),
            pltpu.VMEM((2, 3, 2, rows, columns), f32),
            pltpu.VMEM((2, 3, 2, rows, columns), f32),
            pltpu.VMEM((16, columns), f32),
            pltpu.VMEM((16, columns), f32),
            pltpu.VMEM((4, planes, rows, columns), f32),
            pltpu.VMEM((19, planes + 2, rows, columns), f32),
            pltpu.SemaphoreType.DMA((7,)),
            pltpu.SemaphoreType.DMA((7,)),
        ],
        compiler_params=pltpu.CompilerParams(
            collective_id=0, has_side_effects=True, vmem_limit_bytes=48 * 1024 * 1024
        ),
    )(
        cell_counts,
        up_list,
        down_list,
        distributions,
        cells,
        spread_sites.T,
        stiffness.reshape(1, coefficients),
        basis,
    )
    moved_cells = jnp.transpose(moved[..., :coefficients], (0, 1, 3, 2))
    return (new_distributions, moved_cells)


def solution(mesh):
    placed = (
        P(None, "slab", "half", None),
        P(None, None, None, ("slab", "half")),
        P(("slab", "half")),
        P(("slab", "half")),
        P(("slab", "half")),
        P(None, ("slab", "half")),
        P(),
        P(),
    )
    return jax.shard_map(
        shards,
        mesh=mesh,
        in_specs=placed,
        out_specs=(P(None, "slab", "half", None), P(None, None, None, ("slab", "half"))),
        check_vma=False,
    )
```

time: 85.3 us -> 32.2 us (0.38)
  matrix products: 36.8 us -> 0 us
  Pallas kernels: 0 us -> 26.3 us
  starting transfers between devices: 15.8 us -> 0 us
  waiting for transfers between devices: 15.8 us -> 0 us
  local copies, waits for them, and re-layouts: 9.02 us -> 4.38 us
  other arithmetic: 4.62 us -> 0 us
  loops' own time: 1.43 us -> 0 us
    dot_general x33 -> x0, matrix products: 36.8 us -> none  [the longest x24 28.7 us: visit_rows(): jnp.einsum('crn,nz->crz', weighted, column_hot, precision=full_precision)]
    pallas_call x0 -> x1, Pallas kernels: none -> 26.3 us  [shards(): pl.pallas_call(step_kernel, out_shape=(jax.ShapeDtypeStruct(distributions...]
    ppermute x8 -> x0, starting transfers between devices: 15.8 us -> none  [the longest x4 9.18 us: from_behind(): lax.ppermute(array, axis, [(i, (i + by) % devices) for i in range(devices)])]
    ppermute x8 -> x0, waiting for transfers between devices: 15.8 us -> none  [the longest x2 8.34 us: padded_2(): lax.ppermute(tail, axis, [(i, (i + 1) % count) for i in range(count)])]
    mul x24 -> x0, local copies, waits for them, and re-layouts: 2.22 us -> none  [visit_rows(): weighted = force_piece[:, None, :] * row_hot[None]]
    reshape x24 -> x0, local copies, waits for them, and re-layouts: 1.79 us -> none  [visit_rows(): site_piece = lax.dynamic_slice_in_dim(spread_sites, turn * group_rows, gr...]
    another operation x1 -> x0, loops' own time: 1.43 us -> none  [spread_points(): return lax.fori_loop(0, point_rows // group_rows, visit_rows, empty_total)]
    unnamed x25 -> x15, local copies, waits for them, and re-layouts: 3.13 us -> 4.29 us
  transfers between devices with their start and end apart: 8 -> 0, of which waited for: 6 -> 0; matrix products, arithmetic and copies ran while one was open for 7% -> 0% of each run, Pallas kernels for 0% -> 0%
where the time goes in v2:
time: 32.2 us; the launch traced here: 32 us
  Pallas kernels  26.3 us (82%)
  local copies, waits for them, and re-layouts  4.38 us (14%)
  between operations  1.36 us (4%)
    pallas_call x1, Pallas kernels, shards(): pl.pallas_call(step_kernel, out_shape=(jax.ShapeDtypeStruct(distributions...  26.3 us
    unnamed x15, local copies, waits for them, and re-layouts  4.29 us

profile of v2, /device:TPU:0, one launch (start us, length us, event | category | flops | bytes accessed | tf_op | source)
XLA Modules:
  0.0 32.0 jit_solution(12942022404112031096)
XLA Ops:
  1.3 1.3 %copy.10 = f32[2,3,169,96]{2,3,1,0:T(8,128)S(1)} copy(f32[2,3,169,96]{3,0,2,1:T(2,128)} %param.9) | data formatting | bytes 778752 | tf_op args[1]
  2.6 0.0 copy-start
  2.6 0.0 copy-start.1
  2.6 0.0 copy-start.2
  2.6 0.0 copy-start.3
  2.6 0.0 copy-start.4
  2.6 0.0 copy-start.5
  2.7 0.9 %copy-done = f32[19,2,16,256]{3,2,1,0:T(8,128)S(1)} copy-done((f32[19,2,16,256]{3,2,1,0:T(8,128)S(1)}, f32[19,2,16,256]{3,2,1,0:T(8,128)}, u32[]{:S(2)}) %copy-start) | copy-done | bytes 622616
  3.7 0.1 copy-done.1
  3.7 0.0 copy-done.2
  3.8 0.0 copy-done.3
  3.8 0.0 copy-done.4
  3.8 0.0 copy-done.5
  3.8 26.3 %shard_map.95 = (f32[19,2,16,256]{3,2,1,0:T(8,128)S(1)}, f32[2,3,112,256]{3,2,1,0:T(8,128)S(1)}) custom-call(s32[1]{0:T(128)S(6)} %copy.13.count_ref, s32[8]{0:T(128)S(1)} %copy-done.4, s32[8]{0:T(128)S(1)} %copy-done.5, f32[19,2,16,256]{3,2,1,0:T(8,128)S(1)} %copy-done, f32[2,3,96,256]{3,2,1,0:T(8,128)S(1)} %pad.4.cells_ref, s32[112,384]{1,0:T(8,128)S(1)} %bitcast.5, ...), custom_call_target="tpu_custom_call" | custom-call | tf_op jit(solution)/shard_map/pallas_call | solution.py:365
  30.1 1.1 %copy.11 = f32[2,3,169,112]{3,0,2,1:T(2,128)} copy(f32[2,3,169,112]{2,3,1,0:T(8,128)S(1)} %slice_bitcast_fusion) | data formatting | bytes 908544
  31.2 0.8 %copy.14 = f32[19,2,16,256]{3,2,1,0:T(8,128)} copy(f32[19,2,16,256]{3,2,1,0:T(8,128)S(1)} %get-tuple-element.10) | data formatting | bytes 1245184
  (2 shorter events, 0.1 us)
Async XLA Ops:
  2.6 1.1 %copy-start = (f32[19,2,16,256]{3,2,1,0:T(8,128)S(1)}, f32[19,2,16,256]{3,2,1,0:T(8,128)}, u32[]{:S(2)}) copy-start(f32[19,2,16,256]{3,2,1,0:T(8,128)} %dist_ref.1) | copy-start | bytes 1867780
  2.6 1.1 %copy-start.1 = (f32[169,384]{1,0:T(8,128)S(1)}, f32[169,384]{1,0:T(8,128)}, u32[]{:S(2)}) copy-start(f32[169,384]{1,0:T(8,128)} %basis_ref.1) | copy-start | bytes 778756
  2.6 1.2 %copy-start.2 = (s32[384,112]{0,1:T(8,128)S(1)}, s32[384,112]{0,1:T(8,128)}, u32[]{:S(2)}) copy-start(s32[384,112]{0,1:T(8,128)} %param.13) | copy-start | bytes 516100
  2.6 1.2 %copy-start.3 = (f32[169]{0:T(256)S(1)}, f32[169]{0:T(256)}, u32[]{:S(2)}) copy-start(f32[169]{0:T(256)} %param.14) | copy-start | bytes 2032
  2.6 1.1 %copy-start.4 = (s32[8]{0:T(128)S(1)}, s32[8]{0:T(128)}, u32[]{:S(2)}) copy-start(s32[8]{0:T(128)} %up_ref.1) | copy-start | bytes 100
  2.6 1.1 %copy-start.5 = (s32[8]{0:T(128)S(1)}, s32[8]{0:T(128)}, u32[]{:S(2)}) copy-start(s32[8]{0:T(128)} %down_ref.1) | copy-start | bytes 100

commit v3 on v2

--- a/solution.py
+++ b/solution.py
@@ -89,6 +89,15 @@
 
 def step_kernel(
     count_ref,
+    up_in,
+    down_in,
+    dist_in,
+    cells_in,
+    sites_in,
+    stiff_in,
+    basis_in,
+    out_ref,
+    moved_out_ref,
     up_ref,
     down_ref,
     dist_ref,
@@ -96,7 +105,8 @@
     sites_ref,
     stiff_ref,
     basis_ref,
-    out_ref,
+    load_sems,
+    cells_by_slot,
     moved_ref,
     basis_pad,
     stiff_pad,
@@ -125,13 +135,31 @@
 
     planes, rows, columns = dist_ref.shape[1:]
     coefficients, points = basis_ref.shape
-    capacity, width = cells_ref.shape[2:]
+    capacity, width = cells_by_slot.shape[2:]
     move = up_ref.shape[0]
     slots = sites_ref.shape[0]
+    padded_slots = moved_ref.shape[2]
 
     barrier = pltpu.get_barrier_semaphore()
     for device in (above, below, across):
         pl.semaphore_signal(barrier, inc=1, device_id=device, device_id_type=mesh_ids)
+
+    loads = [
+        pltpu.make_async_copy(source, target, load_sems.at[k])
+        for k, (source, target) in enumerate(
+            (
+                (cells_in, cells_ref),
+                (up_in, up_ref),
+                (down_in, down_ref),
+                (basis_in, basis_ref),
+                (stiff_in, stiff_ref),
+                (dist_in, dist_ref),
+                (sites_in, sites_ref),
+            )
+        )
+    ]
+    for load in loads:
+        load.start()
 
     def remote(at, source, target, device):
         return pltpu.make_async_remote_copy(
@@ -143,6 +171,16 @@
             device_id_type=mesh_ids,
         )
 
+    loads[0].wait()
+    for w in range(2):
+        for c in range(3):
+            cells_by_slot[w, c] = jnp.pad(
+                cells_ref[c, :, w, :],
+                ((0, width - coefficients), (0, padded_slots - capacity)),
+            ).T[:capacity]
+
+    for load in loads[1:3]:
+        load.wait()
     entry_ids = lax.broadcasted_iota(jnp.int32, (2 * move, capacity), 0)
     slot_ids = lax.broadcasted_iota(jnp.int32, (2 * move, capacity), 1)
     entries = jnp.zeros((2 * move, capacity), jnp.int32)
@@ -154,19 +192,15 @@
         for c in range(3):
             picked = jnp.dot(
                 selector,
-                cells_ref[w, c],
+                cells_by_slot[w, c],
                 precision=full_precision,
                 preferred_element_type=jnp.float32,
             )
             cell_send[0, w, c] = picked[:move]
             cell_send[1, w, c] = picked[move:]
 
-    pl.semaphore_wait(barrier, 3)
-    cells_up = remote(0, cell_send.at[0], cell_recv.at[0], above)
-    cells_down = remote(1, cell_send.at[1], cell_recv.at[1], below)
-    cells_up.start()
-    cells_down.start()
-
+    for load in loads[3:]:
+        load.wait()
     for p in range(planes):
         moments = moments_of([dist_ref[i, p] for i in all_ids])
         for k in range(4):
@@ -176,11 +210,6 @@
             halo_send[side, k] = own_moments[k, p]
         for k, i in enumerate(ids):
             halo_send[side, 4 + k] = dist_ref[i, p]
-    halo_up = remote(2, halo_send.at[0], halo_recv.at[0], above)
-    halo_down = remote(3, halo_send.at[1], halo_recv.at[1], below)
-    halo_up.start()
-    halo_down.start()
-
     basis_pad[...] = jnp.zeros_like(basis_pad)
     basis_pad[:coefficients, :] = basis_ref[...]
     stiff_pad[...] = jnp.zeros_like(stiff_pad)
@@ -192,7 +221,7 @@
         gone = gone | (held == up_ref[k]) | (held == down_ref[k])
     for w in range(2):
         for c in range(3):
-            moved_ref[w, c, :capacity, :] = jnp.where(gone, 0.0, cells_ref[w, c])
+            moved_ref[w, c, :capacity, :] = jnp.where(gone, 0.0, cells_by_slot[w, c])
 
     def point_forces(first, count):
         current = [moved_ref[0, c, first : first + count, :] for c in range(3)]
@@ -213,7 +242,7 @@
         for c in range(3):
             pushes[c, first : first + count, :] = parts[3 + c] - factor * radial[c]
 
-    group = 8
+    group = 16
     site_rows = spread_acc.shape[0] // 6
     shift = columns.bit_length() - 1
     zero = jnp.zeros((), jnp.bfloat16)
@@ -259,16 +288,30 @@
         )
         return carry
 
+    early = capacity // group // 3
     spread_acc[...] = jnp.zeros_like(spread_acc)
     point_forces(0, capacity)
-    lax.fori_loop(0, capacity // group, spread, 0)
+    lax.fori_loop(0, early, spread, 0)
+
+    pl.semaphore_wait(barrier, 3)
+    cells_up = remote(0, cell_send.at[0], cell_recv.at[0], above)
+    cells_down = remote(1, cell_send.at[1], cell_recv.at[1], below)
+    cells_up.start()
+    cells_down.start()
+
+    halo_up = remote(2, halo_send.at[0], halo_recv.at[0], above)
+    halo_down = remote(3, halo_send.at[1], halo_recv.at[1], below)
+    halo_up.start()
+    halo_down.start()
+
+    lax.fori_loop(early, capacity // group, spread, 0)
 
     cells_up.wait()
     cells_down.wait()
     for w in range(2):
         for c in range(3):
             moved_ref[w, c, capacity : capacity + move, :] = cell_recv[0, w, c]
-            moved_ref[w, c, capacity + move :, :] = cell_recv[1, w, c]
+            moved_ref[w, c, capacity + move : slots, :] = cell_recv[1, w, c]
     point_forces(capacity, 2 * move)
     lax.fori_loop(capacity // group, slots // group, spread, 0)
 
@@ -284,6 +327,9 @@
     force_up = remote(5, force_own.at[1], force_recv.at[0], above)
     force_down.start()
     force_up.start()
+    for w in range(2):
+        for c in range(3):
+            moved_out_ref[c, :, w, :] = moved_ref[w, c].T[:coefficients, :slots]
     halo_up.wait()
     halo_down.wait()
     force_down.wait()
@@ -355,22 +401,29 @@
     points, slots = spread_sites.shape
     move = up_list.shape[0]
     width = -(-coefficients // 128) * 128
-    cells = jnp.pad(
-        jnp.transpose(cell_states, (0, 1, 3, 2)),
-        ((0, 0), (0, 0), (0, 0), (0, width - coefficients)),
-    )
-    scalars = pl.BlockSpec(memory_space=pltpu.SMEM)
+    padded_slots = -(-slots // 128) * 128
+    anywhere = pl.BlockSpec(memory_space=pltpu.HBM)
     vectors = pl.BlockSpec(memory_space=pltpu.VMEM)
     f32 = jnp.float32
     new_distributions, moved = pl.pallas_call(
         step_kernel,
         out_shape=(
-            jax.ShapeDtypeStruct(distributions.shape, f32),
-            jax.ShapeDtypeStruct((2, 3, slots, width), f32),
+            pltpu.VMEM(distributions.shape, f32),
+            pltpu.VMEM((3, coefficients, 2, slots), f32),
         ),
-        in_specs=[scalars] * 3 + [vectors] * 5,
+        in_specs=[pl.BlockSpec(memory_space=pltpu.SMEM)] + [anywhere] * 7,
         out_specs=(vectors, vectors),
         scratch_shapes=[
+            pltpu.SMEM(up_list.shape, jnp.int32),
+            pltpu.SMEM(down_list.shape, jnp.int32),
+            pltpu.VMEM(distributions.shape, f32),
+            pltpu.VMEM((3, coefficients, 2, capacity), f32),
+            pltpu.VMEM((slots, points), jnp.int32),
+            pltpu.VMEM((1, coefficients), f32),
+            pltpu.VMEM((coefficients, points), f32),
+            pltpu.SemaphoreType.DMA((7,)),
+            pltpu.VMEM((2, 3, capacity, width), f32),
+            pltpu.VMEM((2, 3, padded_slots, width), f32),
             pltpu.VMEM((width, points), f32),
             pltpu.VMEM((1, width), f32),
             pltpu.VMEM((3, slots, points), f32),
@@ -389,19 +442,19 @@
             pltpu.SemaphoreType.DMA((7,)),
         ],
         compiler_params=pltpu.CompilerParams(
-            collective_id=0, has_side_effects=True, vmem_limit_bytes=48 * 1024 * 1024
+            collective_id=0, has_side_effects=True, vmem_limit_bytes=56 * 1024 * 1024
         ),
     )(
         cell_counts,
         up_list,
         down_list,
         distributions,
-        cells,
+        jnp.transpose(cell_states, (1, 2, 0, 3)),
         spread_sites.T,
         stiffness.reshape(1, coefficients),
         basis,
     )
-    moved_cells = jnp.transpose(moved[..., :coefficients], (0, 1, 3, 2))
+    moved_cells = jnp.transpose(moved, (2, 0, 1, 3))
     return (new_distributions, moved_cells)
 
 

time: 32.2 us -> 28.5 us (0.89)
  local copies, waits for them, and re-layouts: 4.38 us -> 1.62 us
  Pallas kernels: 26.3 us -> 25.4 us
    unnamed x15 -> x2, local copies, waits for them, and re-layouts: 4.29 us -> 1.62 us
    pallas_call x1, Pallas kernels: 26.3 us -> 25.4 us  [shards(): pl.pallas_call(step_kernel, out_shape=(pltpu.VMEM(distributions.shape, f3...]
where the time goes in v3:
time: 28.5 us; the launch traced here: 28.3 us
  Pallas kernels  25.4 us (89%)
  local copies, waits for them, and re-layouts  1.62 us (6%)
  between operations  1.29 us (5%)
    pallas_call x1, Pallas kernels, shards(): pl.pallas_call(step_kernel, out_shape=(pltpu.VMEM(distributions.shape, f3...  25.4 us
    unnamed x2, local copies, waits for them, and re-layouts  1.62 us

profile of v3, /device:TPU:0, one launch (start us, length us, event | category | flops | bytes accessed | tf_op | source)
XLA Modules:
  0.0 28.3 jit_solution(10629090051203728960)
XLA Ops:
  1.3 25.4 %shard_map.95 = (f32[19,2,16,256]{3,2,1,0:T(8,128)S(1)}, f32[3,169,2,112]{3,2,1,0:T(2,128)S(1)}) custom-call(s32[1]{0:T(128)S(6)} %copy.14.count_ref, s32[8]{0:T(128)} %up_in.1, s32[8]{0:T(128)} %down_in.1, f32[19,2,16,256]{3,2,1,0:T(8,128)} %dist_in.1, f32[3,169,2,96]{3,2,1,0:T(2,128)} %bitcast.5, s32[112,384]{1,0:T(8,128)} %bitcast.6, f32[1,169]{1,0:T(1,128)} %bitcast.7, ...), custom_call_target="tpu_custom_call" | custom-call | tf_op jit(solution)/shard_map/pallas_call | solution.py:408
  26.7 0.8 %copy.12 = f32[19,2,16,256]{3,2,1,0:T(8,128)} copy(f32[19,2,16,256]{3,2,1,0:T(8,128)S(1)} %get-tuple-element.6) | data formatting | bytes 1245184
  27.6 0.8 %copy.13 = f32[2,3,169,112]{3,0,2,1:T(2,128)} copy(f32[2,3,169,112]{3,0,2,1:T(2,128)S(1)} %bitcast.4) | data formatting | bytes 908544

commit v4 on v3

--- a/solution.py
+++ b/solution.py
@@ -335,20 +335,42 @@
     force_down.wait()
     force_up.wait()
 
-    for plane in range(planes + 2):
+    def collided(plane, ids, span):
         side, at = divmod(plane, 2)
-        force = [force_own[side, c, at] + force_recv[side, c, at] for c in range(3)]
+        force = [
+            force_own[side, c, at, span, :] + force_recv[side, c, at, span, :] for c in range(3)
+        ]
         if plane == 0 or plane == planes + 1:
             which = 0 if plane == 0 else 1
-            ids = ahead_ids if plane == 0 else behind_ids
-            moments = [halo_recv[which, k] for k in range(4)]
-            found = collide(
-                ids, lambda i: halo_recv[which, 4 + ids.index(i)], moments, force
-            )
-        else:
-            moments = [own_moments[k, plane - 1] for k in range(4)]
-            found = collide(all_ids, lambda i: dist_ref[i, plane - 1], moments, force)
-        for i, value in found.items():
+            sent = ahead_ids if plane == 0 else behind_ids
+            ids = [i for i in ids if i in sent]
+            moments = [halo_recv[which, k, span, :] for k in range(4)]
+            return collide(
+                ids, lambda i: halo_recv[which, 4 + sent.index(i), span, :], moments, force
+            )
+        moments = [own_moments[k, plane - 1, span, :] for k in range(4)]
+        return collide(ids, lambda i: dist_ref[i, plane - 1, span, :], moments, force)
+
+    border = pl.ds(pl.multiple_of((1 - half) * (rows - 8), 8), 8)
+    lower_half = jnp.full((1, columns), half, jnp.int32) == 0
+    edge = [collided(plane, rising_ids + falling_ids, border) for plane in range(planes + 2)]
+
+    def edge_row(i, p, at):
+        vel = lattice_velocities[i]
+        value = edge[p + 1 - vel[0]][i]
+        if vel[2]:
+            value = pltpu.roll(value, vel[2] % columns, 1)
+        return value[at : at + 1]
+
+    for j, (i, o) in enumerate(zip(rising_ids, falling_ids)):
+        for p in range(planes):
+            at = j * planes + p
+            row_send[at : at + 1, :] = jnp.where(lower_half, edge_row(i, p, 7), edge_row(o, p, 0))
+    rows_across = remote(6, row_send, row_recv, across)
+    rows_across.start()
+
+    for plane in range(planes + 2):
+        for i, value in collided(plane, all_ids, slice(0, rows)).items():
             relaxed[i, plane] = value
 
     def carried(i, p):
@@ -359,19 +381,14 @@
         return value
 
     row_ids = lax.broadcasted_iota(jnp.int32, (rows, columns), 0)
-    lower_half = jnp.full((1, columns), half, jnp.int32) == 0
     for j, (i, o) in enumerate(zip(rising_ids, falling_ids)):
         for p in range(planes):
             rising = carried(i, p)
             falling = carried(o, p)
-            at = j * planes + p
-            row_send[at : at + 1, :] = jnp.where(lower_half, rising[rows - 1 :], falling[:1])
             out_ref[i, p] = jnp.where(row_ids == 0, relaxed[o, p + 1], pltpu.roll(rising, 1, 0))
             out_ref[o, p] = jnp.where(
                 row_ids == rows - 1, relaxed[i, p + 1], pltpu.roll(falling, rows - 1, 0)
             )
-    rows_across = remote(6, row_send, row_recv, across)
-    rows_across.start()
     for i in level_ids:
         for p in range(planes):
             out_ref[i, p] = carried(i, p)

time: 28.5 us -> 28.2 us (0.989)
  no operation moved by 1% of the time
where the time goes in v4:
time: 28.2 us; the launch traced here: 28.1 us
  Pallas kernels  25.2 us (89%)
  local copies, waits for them, and re-layouts  1.62 us (6%)
  between operations  1.29 us (5%)
    pallas_call x1, Pallas kernels, shards(): pl.pallas_call(step_kernel, out_shape=(pltpu.VMEM(distributions.shape, f3...  25.2 us
    unnamed x2, local copies, waits for them, and re-layouts  1.62 us

profile of v4, /device:TPU:0, one launch (start us, length us, event | category | flops | bytes accessed | tf_op | source)
XLA Modules:
  0.0 28.1 jit_solution(13447056068972134663)
XLA Ops:
  1.3 25.2 %shard_map.95 = (f32[19,2,16,256]{3,2,1,0:T(8,128)S(1)}, f32[3,169,2,112]{3,2,1,0:T(2,128)S(1)}) custom-call(s32[1]{0:T(128)S(6)} %copy.14.count_ref, s32[8]{0:T(128)} %up_in.1, s32[8]{0:T(128)} %down_in.1, f32[19,2,16,256]{3,2,1,0:T(8,128)} %dist_in.1, f32[3,169,2,96]{3,2,1,0:T(2,128)} %bitcast.5, s32[112,384]{1,0:T(8,128)} %bitcast.6, f32[1,169]{1,0:T(1,128)} %bitcast.7, ...), custom_call_target="tpu_custom_call" | custom-call | tf_op jit(solution)/shard_map/pallas_call | solution.py:425
  26.5 0.8 %copy.12 = f32[19,2,16,256]{3,2,1,0:T(8,128)} copy(f32[19,2,16,256]{3,2,1,0:T(8,128)S(1)} %get-tuple-element.6) | data formatting | bytes 1245184
  27.3 0.8 %copy.13 = f32[2,3,169,112]{3,0,2,1:T(2,128)} copy(f32[2,3,169,112]{3,0,2,1:T(2,128)S(1)} %bitcast.4) | data formatting | bytes 908544
